TPU v7x, 32 devices: a whole 2x2x4 slice. The times are simulated.
32 devices in a mesh: gx: 4 (over z), gy: 8 (over y, x, core).
Axes of the slice: x: 2, y: 2, z: 4, core: 2. Of those that a mesh axis runs over, the one named last changes fastest.
Arguments:
- hidden: float32 [16384, 1024], P(('gx', 'gy')), may hold values from -6 to 6
- memory: bfloat16 [18816, 1024], P(('gx', 'gy')), may hold values from -6 to 6
- lengths: int32 [32], P(('gx', 'gy')), may hold values from 192 to 512, as said below
- page_class: int32 [32], P(('gx', 'gy')), may hold values from 0 to 1
- cotangent: float32 [16384, 1024], P(('gx', 'gy')), may hold values from -6 to 6
- w_self_qkv: bfloat16 [1024, 3072], P(('gx', 'gy')), may hold values from -0.1875 to 0.1875
- w_self_out: bfloat16 [1024, 1024], P(('gx', 'gy')), may hold values from -3 to 3
- w_cross_q: bfloat16 [1024, 1024], P(('gx', 'gy')), may hold values from -0.1875 to 0.1875
- w_cross_kv: bfloat16 [1024, 2048], P(('gx', 'gy')), may hold values from -0.1875 to 0.1875
- w_cross_out: bfloat16 [1024, 1024], P(('gx', 'gy')), may hold values from -3 to 3
- w_fc1: bfloat16 [1024, 4096], P(('gx', 'gy')), may hold values from -0.1875 to 0.1875
- w_fc2: bfloat16 [4096, 1024], P(('gx', 'gy')), may hold values from -0.09375 to 0.09375
- norm_gains: bfloat16 [3, 1024], P(None, ('gx', 'gy')), may hold values from 0.5 to 1.5
- norm_biases: bfloat16 [3, 1024], P(None, ('gx', 'gy')), may hold values from -1.75 to 1.75
Outputs:
- result: float32 [16384, 1024], P(('gx', 'gy'))
- grad_hidden: float32 [16384, 1024], P(('gx', 'gy'))
- grad_memory: float32 [18816, 1024], P(('gx', 'gy'))
- grad_self_qkv: float32 [1024, 3072], P(('gx', 'gy'))
- grad_self_out: float32 [1024, 1024], P(('gx', 'gy'))
- grad_cross_q: float32 [1024, 1024], P(('gx', 'gy'))
- grad_cross_kv: float32 [1024, 2048], P(('gx', 'gy'))
- grad_cross_out: float32 [1024, 1024], P(('gx', 'gy'))
- grad_fc1: float32 [1024, 4096], P(('gx', 'gy'))
- grad_fc2: float32 [4096, 1024], P(('gx', 'gy'))
- grad_gains: float32 [3, 1024], P(None, ('gx', 'gy'))
- grad_biases: float32 [3, 1024], P(None, ('gx', 'gy'))
Inputs may be any that keep to these rules, and one draw needn't show every extreme that they name: `lengths`: some page has exactly 512 decoder tokens; every page has at least 192.
All inputs are finite; a program needn't handle non-finite values.
Results may differ from a plain program's by a relative error of at most 0.017.
Values may be sent and summed in bfloat16 or wider, within the bound.
No kernel may reach another device: no remote copies, remote signals or barrier semaphores. Data moves between devices by JAX's collectives and lax.ppermute only.
A program may use at most 320 MiB of HBM per device.

v0:
```python
import jax
import jax.numpy as jnp
from jax import lax
from jax.sharding import PartitionSpec as P

D = 1024
HEADS = 16
LSLOT = 512
MEM_BIG = 588


def layer_norm(v, gain_row, bias_row):
    center = v - jnp.mean(v, -1, keepdims=True)
    variance = jnp.mean(center * center, -1, keepdims=True)
    return center * lax.rsqrt(variance + 1e-05) * gain_row + bias_row


def gelu_exact(v):
    return jax.nn.gelu(v, approximate=False)


def matmul(a, b):
    return jnp.dot(a, b, preferred_element_type=jnp.float32)


def matmul_tn(a, b):
    return lax.dot_general(a, b, (((0,), (0,)), ((), ())), preferred_element_type=jnp.float32)


def matmul_nt(a, b):
    return lax.dot_general(a, b, (((1,), (1,)), ((), ())), preferred_element_type=jnp.float32)


def split_heads(a):
    return a.reshape(a.shape[0], HEADS, a.shape[1] // HEADS)


def attn_scores(query, key_rows, allowed):
    scale = (query.shape[1] // HEADS) ** (-0.5)
    scores = (
        jnp.einsum(
            "qhd,khd->hqk",
            split_heads(query),
            split_heads(key_rows),
            preferred_element_type=jnp.float32,
        )
        * scale
    )
    return jnp.where(allowed[None], scores, -1e30)


def attend_forward(query, key_rows, values, allowed):
    scores = attn_scores(query, key_rows, allowed)
    row_top = jnp.max(scores, -1, keepdims=True)
    expd = jnp.exp(scores - row_top)
    totals = jnp.sum(expd, -1, keepdims=True)
    probs_low = (expd / totals).astype(jnp.bfloat16)
    mixed = jnp.einsum(
        "hqk,khd->qhd", probs_low, split_heads(values), preferred_element_type=jnp.float32
    )
    return (mixed.reshape(query.shape[0], -1).astype(jnp.bfloat16), row_top + jnp.log(totals))


def attend_backward(query, key_rows, values, grad_mixed, log_total, allowed):
    scale = (query.shape[1] // HEADS) ** (-0.5)
    probs = jnp.exp(attn_scores(query, key_rows, allowed) - log_total)
    probs_low = probs.astype(jnp.bfloat16)
    grad_heads = split_heads(grad_mixed)
    grad_values = jnp.einsum(
        "hqk,qhd->khd", probs_low, grad_heads, preferred_element_type=jnp.float32
    )
    grad_probs = jnp.einsum(
        "qhd,khd->hqk", grad_heads, split_heads(values), preferred_element_type=jnp.float32
    )
    inner = jnp.sum(grad_probs * probs, -1, keepdims=True)
    grad_scores = (probs * (grad_probs - inner)).astype(jnp.bfloat16)
    grad_query = (
        jnp.einsum(
            "hqk,khd->qhd", grad_scores, split_heads(key_rows), preferred_element_type=jnp.float32
        )
        * scale
    )
    grad_keys = (
        jnp.einsum(
            "hqk,qhd->khd", grad_scores, split_heads(query), preferred_element_type=jnp.float32
        )
        * scale
    )
    return (
        grad_query.reshape(query.shape[0], -1).astype(jnp.bfloat16),
        grad_keys.reshape(key_rows.shape[0], -1).astype(jnp.bfloat16),
        grad_values.reshape(key_rows.shape[0], -1).astype(jnp.bfloat16),
    )


def self_allowed(length):
    position = jnp.arange(LSLOT)
    return (position[None, :] <= position[:, None]) & (position[None, :] < length)


def cross_allowed(slots_used):
    slots = jnp.arange(MEM_BIG)
    return jnp.broadcast_to(slots[None, :] < slots_used, (LSLOT, MEM_BIG))


def self_forward(entry):
    query, key_rows, values, length = entry
    return attend_forward(query, key_rows, values, self_allowed(length))


def cross_forward(entry):
    query, key_rows, values, slots_used = entry
    return attend_forward(query, key_rows, values, cross_allowed(slots_used))


def self_backward(entry):
    query, key_rows, values, grad_mixed, log_total, length = entry
    return attend_backward(query, key_rows, values, grad_mixed, log_total, self_allowed(length))


def cross_backward(entry):
    query, key_rows, values, grad_mixed, log_total, slots_used = entry
    return attend_backward(
        query, key_rows, values, grad_mixed, log_total, cross_allowed(slots_used)
    )


def collect_forward(wa, wb, wc, wd, we, wf, wg, gain_rows, bias_rows):
    return (
        lax.all_gather(wa, ("gx", "gy"), axis=0, tiled=True),
        lax.all_gather(wb, ("gx", "gy"), axis=0, tiled=True),
        lax.all_gather(wc, ("gx", "gy"), axis=0, tiled=True),
        lax.all_gather(wd, ("gx", "gy"), axis=0, tiled=True),
        lax.all_gather(we, ("gx", "gy"), axis=0, tiled=True),
        lax.all_gather(wf, ("gx", "gy"), axis=0, tiled=True),
        lax.all_gather(wg, ("gx", "gy"), axis=0, tiled=True),
        lax.all_gather(gain_rows, ("gx", "gy"), axis=1, tiled=True),
        lax.all_gather(bias_rows, ("gx", "gy"), axis=1, tiled=True),
    )


def collect_backward(wa, wb, wc, wd, we, wf, wg, gain_rows, bias_rows):
    return (
        lax.all_gather(wa, ("gx", "gy"), axis=0, tiled=True),
        lax.all_gather(wb, ("gx", "gy"), axis=0, tiled=True),
        lax.all_gather(wc, ("gx", "gy"), axis=0, tiled=True),
        lax.all_gather(wd, ("gx", "gy"), axis=0, tiled=True),
        lax.all_gather(we, ("gx", "gy"), axis=0, tiled=True),
        lax.all_gather(wf, ("gx", "gy"), axis=0, tiled=True),
        lax.all_gather(wg, ("gx", "gy"), axis=0, tiled=True),
        lax.all_gather(gain_rows, ("gx", "gy"), axis=1, tiled=True),
        lax.all_gather(bias_rows, ("gx", "gy"), axis=1, tiled=True),
    )


def spread_grads(ga, gb, gc, gd, ge, gf, gg, gain_grad, bias_grad):
    return (
        lax.psum_scatter(ga, ("gx", "gy"), scatter_dimension=0, tiled=True),
        lax.psum_scatter(gb, ("gx", "gy"), scatter_dimension=0, tiled=True),
        lax.psum_scatter(gc, ("gx", "gy"), scatter_dimension=0, tiled=True),
        lax.psum_scatter(gd, ("gx", "gy"), scatter_dimension=0, tiled=True),
        lax.psum_scatter(ge, ("gx", "gy"), scatter_dimension=0, tiled=True),
        lax.psum_scatter(gf, ("gx", "gy"), scatter_dimension=0, tiled=True),
        lax.psum_scatter(gg, ("gx", "gy"), scatter_dimension=0, tiled=True),
        lax.psum_scatter(gain_grad, ("gx", "gy"), scatter_dimension=1, tiled=True),
        lax.psum_scatter(bias_grad, ("gx", "gy"), scatter_dimension=1, tiled=True),
    )


def shards(
    hidden,
    memory,
    lengths,
    page_class,
    cotangent,
    w_self_qkv,
    w_self_out,
    w_cross_q,
    w_cross_kv,
    w_cross_out,
    w_fc1,
    w_fc2,
    norm_gains,
    norm_biases,
):
    gathered = collect_forward(
        w_self_qkv,
        w_self_out,
        w_cross_q,
        w_cross_kv,
        w_cross_out,
        w_fc1,
        w_fc2,
        norm_gains,
        norm_biases,
    )
    wqkv, wso, wcq, wckv, wco, wup, wdown, gains_low, biases_low = gathered
    gains = gains_low.astype(jnp.float32)
    biases = biases_low.astype(jnp.float32)
    page_count = lengths.shape[0]
    slots_used = jnp.where(page_class == 0, MEM_BIG, MEM_BIG // 4)
    h1 = layer_norm(hidden, gains[0], biases[0]).astype(jnp.bfloat16)
    qkv = matmul(h1, wqkv).astype(jnp.bfloat16)
    queries = qkv[:, :D].reshape(page_count, LSLOT, D)
    key_rows = qkv[:, D : 2 * D].reshape(page_count, LSLOT, D)
    values = qkv[:, 2 * D :].reshape(page_count, LSLOT, D)
    mixed, self_log = lax.map(self_forward, (queries, key_rows, values, lengths))
    mixed_flat = mixed.reshape(-1, D)
    x1 = hidden + matmul(mixed_flat, wso)
    h2 = layer_norm(x1, gains[1], biases[1]).astype(jnp.bfloat16)
    cross_query = matmul(h2, wcq).astype(jnp.bfloat16)
    kvc = matmul(memory, wckv).astype(jnp.bfloat16)
    cross_q3 = cross_query.reshape(page_count, LSLOT, D)
    cross_k3 = kvc[:, :D].reshape(page_count, MEM_BIG, D)
    cross_v3 = kvc[:, D:].reshape(page_count, MEM_BIG, D)
    mixed_cross, cross_log = lax.map(cross_forward, (cross_q3, cross_k3, cross_v3, slots_used))
    cross_flat = mixed_cross.reshape(-1, D)
    x2 = x1 + matmul(cross_flat, wco)
    h3 = layer_norm(x2, gains[2], biases[2]).astype(jnp.bfloat16)
    upper = matmul(h3, wup)
    activated = gelu_exact(upper).astype(jnp.bfloat16)
    result = x2 + matmul(activated, wdown)
    weights_back = collect_backward(
        w_self_qkv,
        w_self_out,
        w_cross_q,
        w_cross_kv,
        w_cross_out,
        w_fc1,
        w_fc2,
        norm_gains,
        norm_biases,
    )
    bqkv, bso, bcq, bckv, bco, bup, bdown, bgain_low, bbias_low = weights_back
    position = jnp.arange(LSLOT)
    valid = (position[None, :] < lengths[:, None]).reshape(-1)
    grad_out = cotangent * valid[:, None].astype(jnp.float32)
    grad_y3 = grad_out.astype(jnp.bfloat16)
    grad_down = matmul_tn(activated, grad_y3)
    grad_act = matmul_nt(grad_y3, bdown)
    _, gelu_pullback = jax.vjp(gelu_exact, upper)
    grad_upper = gelu_pullback(grad_act)[0].astype(jnp.bfloat16)
    grad_up = matmul_tn(h3, grad_upper)
    grad_h3 = matmul_nt(grad_upper, bup)
    _, norm3_pullback = jax.vjp(layer_norm, x2, gains[2], biases[2])
    grad_from3, gain_grad3, bias_grad3 = norm3_pullback(grad_h3)
    grad_x2 = grad_out + grad_from3
    grad_y2 = grad_x2.astype(jnp.bfloat16)
    grad_cross_out = matmul_tn(cross_flat, grad_y2)
    grad_mixed_cross = matmul_nt(grad_y2, bco).astype(jnp.bfloat16).reshape(page_count, LSLOT, D)
    grad_cq, grad_ck, grad_cv = lax.map(
        cross_backward, (cross_q3, cross_k3, cross_v3, grad_mixed_cross, cross_log, slots_used)
    )
    grad_cross_query = grad_cq.reshape(-1, D)
    grad_kvc = jnp.concatenate([grad_ck.reshape(-1, D), grad_cv.reshape(-1, D)], axis=1)
    grad_cross_q = matmul_tn(h2, grad_cross_query)
    grad_cross_kv = matmul_tn(memory, grad_kvc)
    grad_memory = matmul_nt(grad_kvc, bckv)
    grad_h2 = matmul_nt(grad_cross_query, bcq)
    _, norm2_pullback = jax.vjp(layer_norm, x1, gains[1], biases[1])
    grad_from2, gain_grad2, bias_grad2 = norm2_pullback(grad_h2)
    grad_x1 = grad_x2 + grad_from2
    grad_y1 = grad_x1.astype(jnp.bfloat16)
    grad_self_out = matmul_tn(mixed_flat, grad_y1)
    grad_mixed = matmul_nt(grad_y1, bso).astype(jnp.bfloat16).reshape(page_count, LSLOT, D)
    grad_sq, grad_sk, grad_sv = lax.map(
        self_backward, (queries, key_rows, values, grad_mixed, self_log, lengths)
    )
    grad_qkv = jnp.concatenate(
        [grad_sq.reshape(-1, D), grad_sk.reshape(-1, D), grad_sv.reshape(-1, D)], axis=1
    )
    grad_self_qkv = matmul_tn(h1, grad_qkv)
    grad_h1 = matmul_nt(grad_qkv, bqkv)
    _, norm1_pullback = jax.vjp(layer_norm, hidden, gains[0], biases[0])
    grad_from1, gain_grad1, bias_grad1 = norm1_pullback(grad_h1)
    grad_hidden = grad_x1 + grad_from1
    gain_grads = jnp.stack([gain_grad1, gain_grad2, gain_grad3])
    bias_grads = jnp.stack([bias_grad1, bias_grad2, bias_grad3])
    owned = spread_grads(
        grad_self_qkv,
        grad_self_out,
        grad_cross_q,
        grad_cross_kv,
        grad_cross_out,
        grad_up,
        grad_down,
        gain_grads,
        bias_grads,
    )
    return (
        result,
        grad_hidden,
        grad_memory,
        owned[0],
        owned[1],
        owned[2],
        owned[3],
        owned[4],
        owned[5],
        owned[6],
        owned[7],
        owned[8],
    )


def solution(mesh):
    return jax.shard_map(
        shards,
        mesh=mesh,
        in_specs=(
            P(("gx", "gy"), None),
            P(("gx", "gy"), None),
            P(("gx", "gy")),
            P(("gx", "gy")),
            P(("gx", "gy"), None),
            P(("gx", "gy"), None),
            P(("gx", "gy"), None),
            P(("gx", "gy"), None),
            P(("gx", "gy"), None),
            P(("gx", "gy"), None),
            P(("gx", "gy"), None),
            P(("gx", "gy"), None),
            P(None, ("gx", "gy")),
            P(None, ("gx", "gy")),
        ),
        out_specs=(
            P(("gx", "gy"), None),
            P(("gx", "gy"), None),
            P(("gx", "gy"), None),
            P(("gx", "gy"), None),
            P(("gx", "gy"), None),
            P(("gx", "gy"), None),
            P(("gx", "gy"), None),
            P(("gx", "gy"), None),
            P(("gx", "gy"), None),
            P(("gx", "gy"), None),
            P(None, ("gx", "gy")),
            P(None, ("gx", "gy")),
        ),
        check_vma=False,
    )
```

profile of v0, /device:TPU:0, one launch (start us, length us, event | category | flops | bytes accessed | tf_op | source)
XLA Modules:
  0.0 1965.6 jit_solution(9670675433567401931)
XLA Ops:
  16.6 43.2 %all-gather = bf16[32,32,3]{1,2,0:T(4,128)(2,1)S(1)} all-gather(bf16[1,32,3]{1,2,0:T(4,128)(2,1)S(1)} %bitcast.175), channel_id=1, replica_groups=mesh['gx'=4,'gy'=8] {'gx','gy'}, dimensions={0}, use_global_device_ids=true | all-gather | bytes 6336 | tf_op jit(solution)/shard_map/all_gather | solution.py:137
  60.0 36.8 %all-gather.1 = bf16[32,32,3]{1,2,0:T(4,128)(2,1)S(1)} all-gather(bf16[1,32,3]{1,2,0:T(4,128)(2,1)S(1)} %bitcast.176), channel_id=1, replica_groups=mesh['gx'=4,'gy'=8] {'gx','gy'}, dimensions={0}, use_global_device_ids=true | all-gather | bytes 6336 | tf_op jit(solution)/shard_map/all_gather | solution.py:138
  97.8 5.1 convolution_convert_fusion.1
  104.5 2.4 copy.85
  106.9 2.4 copy.83
  109.3 37.4 %all-gather.10.cloned.1.call-done = bf16[1024,3072]{1,0:T(8,128)(2,1)} async-done(((bf16[32,3072]{1,0:T(8,128)(2,1)}), bf16[1024,3072]{1,0:T(8,128)(2,1)}) %all-gather.10.cloned.1.call-update) | async-done | bytes 6291472 | tf_op jit(solution)/shard_map/all_gather | solution.py:130
  146.7 6.7 convolution_convert_fusion
  155.1 2.3 copy.81
  157.4 2.3 copy.80
  159.7 2.3 copy.79
  162.0 10.0 fusion.57
  172.0 8.4 fusion.2
  180.4 8.7 fusion.22
  189.1 15.4 all-gather.12.cloned.1.call-done
  204.5 3.3 fusion.58
  209.5 53.0 %all-gather.16.cloned.1.call-done = bf16[1024,1024]{1,0:T(8,128)(2,1)} async-done(((bf16[32,1024]{1,0:T(8,128)(2,1)}), bf16[1024,1024]{1,0:T(8,128)(2,1)}) %all-gather.16.cloned.1.call-update) | async-done | bytes 2097168 | tf_op jit(solution)/shard_map/all_gather | solution.py:132
  262.5 4.6 convolution_convert_fusion.4
  267.1 2.3 copy.84
  269.4 11.8 fusion.59
  281.2 9.3 fusion
  290.5 10.0 fusion.23
  300.5 19.9 %all-gather.18.cloned.1.call-done = bf16[1024,1024]{1,0:T(8,128)(2,1)} async-done(((bf16[32,1024]{1,0:T(8,128)(2,1)}), bf16[1024,1024]{1,0:T(8,128)(2,1)}) %all-gather.18.cloned.1.call-update) | async-done | bytes 2097168 | tf_op jit(solution)/shard_map/all_gather | solution.py:134
  320.5 3.9 fusion.60
  326.1 73.4 %all-gather.20.cloned.1.call-done = bf16[1024,4096]{1,0:T(8,128)(2,1)} async-done(((bf16[32,4096]{1,0:T(8,128)(2,1)}), bf16[1024,4096]{1,0:T(8,128)(2,1)}) %all-gather.20.cloned.1.call-update) | async-done | bytes 8388624 | tf_op jit(solution)/shard_map/all_gather | solution.py:135
  399.5 26.7 %multiply_convert_fusion.2 = (bf16[512,4096]{1,0:T(8,128)(2,1)}, f32[512,4096]{1,0:T(8,128)}, f32[512,4096]{1,0:T(8,128)}) fusion(bf16[1024,4096]{1,0:T(8,128)(2,1)} %all-gather.20.cloned.1.call-done, f32[512,1024]{1,0:T(8,128)} %copy-done.11, f32[1024]{0:T(1024)S(1)} %bitcast.169, f32[1024]{0:T(1024)S(1)} %bitcast.155, f32[512]{0:T(512)S(1)} %fusion.38, ...), kind=kOutput, calls=%fused_computation.24 | convolution fusion | flops 4433903616 | bytes 31469568 | tf_op jit(solution)/shard_map/dot_general | solution.py:23
  426.3 52.2 %all-gather.22.cloned.1.call-done = bf16[4096,1024]{1,0:T(8,128)(2,1)} async-done(((bf16[128,1024]{1,0:T(8,128)(2,1)}), bf16[4096,1024]{1,0:T(8,128)(2,1)}) %all-gather.22.cloned.1.call-update) | async-done | bytes 8388624 | tf_op jit(solution)/shard_map/all_gather | solution.py:136
  478.5 14.8 add_convert_fusion
  493.3 8.9 multiply_reduce_fusion.2
  506.1 2.3 convolution_convert_fusion.3
  508.4 2.3 copy.86
  510.7 13.1 multiply_reduce_fusion
  523.8 14.0 multiply_convert_fusion
  537.9 1.8 multiply_convert_fusion.6
  539.7 2.9 copy-done.1
  543.3 1.8 multiply_reduce_fusion.3
  548.4 2.3 convolution_convert_fusion.2
  550.7 2.3 copy.87
  553.0 8.9 fusion.24
  561.9 11.6 multiply_reduce_fusion.1
  573.5 12.2 multiply_convert_fusion.1
  585.7 2.6 multiply_convert_fusion.4
  591.3 5.4 multiply_reduce_fusion.4
  598.9 5.2 fusion.33
  604.8 5.4 fusion.46
  610.3 4.5 fusion.30
  615.0 7.1 multiply_convert_fusion.3
  622.1 10.0 fusion.19
  633.2 7.0 convolution_bitcast_fusion
  640.2 9.2 copy.96
  650.1 10.8 fusion.27
  661.5 13.3 fusion.47
  675.1 13.2 fusion.44
  689.0 3.1 fusion.49
  694.7 4.5 fusion.18
  699.3 5.9 convolution_add_fusion.2
  705.2 25.2 %reduce-scatter.32.cloned.1.call-done = f32[32,3]{1,0:T(8,128)} async-done(((f32[1024,3]{1,0:T(8,128)}), f32[32,3]{1,0:T(8,128)}) %reduce-scatter.32.cloned.1.call-update) | async-done | bytes 400
  731.8 130.6 %reduce-scatter.30.cloned.1.call-done = f32[32,3]{1,0:T(8,128)} async-done(((f32[1024,3]{1,0:T(8,128)}), f32[32,3]{1,0:T(8,128)}) %reduce-scatter.30.cloned.1.call-update) | async-done | bytes 400
  863.7 138.5 %reduce-scatter.22.cloned.1.call-done = f32[32,1024]{1,0:T(8,128)} async-done(((f32[1024,1024]{1,0:T(8,128)}), f32[32,1024]{1,0:T(8,128)}) %reduce-scatter.22.cloned.1.call-update) | async-done | bytes 131088 | tf_op jit(solution)/shard_map/reduce_scatter | solution.py:162
  1002.2 139.7 %reduce-scatter.20.cloned.1.call-done = f32[32,1024]{1,0:T(8,128)} async-done(((f32[1024,1024]{1,0:T(8,128)}), f32[32,1024]{1,0:T(8,128)}) %reduce-scatter.20.cloned.1.call-update) | async-done | bytes 131088 | tf_op jit(solution)/shard_map/reduce_scatter | solution.py:160
  1141.9 139.5 %reduce-scatter.18.cloned.1.call-done = f32[32,1024]{1,0:T(8,128)} async-done(((f32[1024,1024]{1,0:T(8,128)}), f32[32,1024]{1,0:T(8,128)}) %reduce-scatter.18.cloned.1.call-update) | async-done | bytes 131088 | tf_op jit(solution)/shard_map/reduce_scatter | solution.py:159
  1281.5 147.5 %reduce-scatter.28.cloned.1.call-done = f32[32,2048]{1,0:T(8,128)} async-done(((f32[1024,2048]{1,0:T(8,128)}), f32[32,2048]{1,0:T(8,128)}) %reduce-scatter.28.cloned.1.call-update) | async-done | bytes 262160
  1428.9 157.7 %reduce-scatter.16.cloned.1.call-done = f32[32,3072]{1,0:T(8,128)} async-done(((f32[1024,3072]{1,0:T(8,128)}), f32[32,3072]{1,0:T(8,128)}) %reduce-scatter.16.cloned.1.call-update) | async-done | bytes 393232 | tf_op jit(solution)/shard_map/reduce_scatter | solution.py:158
  1586.7 184.8 %reduce-scatter.24.cloned.1.call-done = f32[32,4096]{1,0:T(8,128)} async-done(((f32[1024,4096]{1,0:T(8,128)}), f32[32,4096]{1,0:T(8,128)}) %reduce-scatter.24.cloned.1.call-update) | async-done | bytes 524304 | tf_op jit(solution)/shard_map/reduce_scatter | solution.py:163
  1771.4 187.3 %reduce-scatter.26.cloned.1.call-done = f32[128,1024]{1,0:T(8,128)} async-done(((f32[4096,1024]{1,0:T(8,128)}), f32[128,1024]{1,0:T(8,128)}) %reduce-scatter.26.cloned.1.call-update) | async-done | bytes 524304 | tf_op jit(solution)/shard_map/reduce_scatter | solution.py:164
  (198 shorter events, 38.4 us)
Async XLA Ops:
  7.2 90.6 %copy-start = (bf16[588,1024]{1,0:T(8,128)(2,1)S(1)}, bf16[588,1024]{1,0:T(8,128)(2,1)}, u32[]{:S(2)}) copy-start(bf16[588,1024]{1,0:T(8,128)(2,1)} %param.15) | copy-start | bytes 3612676
  7.2 8.5 copy-start.2
  7.2 9.4 copy-start.50
  7.2 52.8 %copy-start.51 = (bf16[3,32]{1,0:T(4,128)(2,1)S(1)}, bf16[3,32]{1,0:T(4,128)(2,1)}, u32[]{:S(2)}) copy-start(bf16[3,32]{1,0:T(4,128)(2,1)} %param.27) | copy-start | bytes 580
  7.2 90.5 %all-gather.14.cloned.1.call-start = ((), (), s32[]{:S(2)}) async-start(), calls=%async_computation.11 | async-start | bytes 4325376 | tf_op jit(solution)/shard_map/all_gather | solution.py:133
  8.0 138.8 %all-gather.10.cloned.1.call-start = ((), (), s32[]{:S(2)}) async-start(), calls=%async_computation.9 | async-start | bytes 6488064 | tf_op jit(solution)/shard_map/all_gather | solution.py:130
  8.7 195.8 %all-gather.12.cloned.1.call-start = ((), (), s32[]{:S(2)}) async-start(), calls=%async_computation.10 | async-start | bytes 2162688 | tf_op jit(solution)/shard_map/all_gather | solution.py:131
  9.4 253.0 %all-gather.16.cloned.1.call-start = ((), (), s32[]{:S(2)}) async-start(), calls=%async_computation.12 | async-start | bytes 2162688 | tf_op jit(solution)/shard_map/all_gather | solution.py:132
  10.0 310.4 %all-gather.18.cloned.1.call-start = ((), (), s32[]{:S(2)}) async-start(), calls=%async_computation.13 | async-start | bytes 2162688 | tf_op jit(solution)/shard_map/all_gather | solution.py:134
  10.6 388.9 %all-gather.20.cloned.1.call-start = ((), (), s32[]{:S(2)}) async-start(), calls=%async_computation.14 | async-start | bytes 8650752 | tf_op jit(solution)/shard_map/all_gather | solution.py:135
  11.2 467.3 %all-gather.22.cloned.1.call-start = ((), (), s32[]{:S(2)}) async-start(), calls=%async_computation.15 | async-start | bytes 8650752 | tf_op jit(solution)/shard_map/all_gather | solution.py:136
  11.9 718.5 %reduce-scatter.32.cloned.1.call-start = ((), (), s32[]{:S(2)}) async-start(), calls=%async_computation.24 | async-start | bytes 540672
  15.7 131.1 %copy-start.27 = (f32[512]{0:T(512)}, f32[512]{0:T(512)S(1)}, u32[]{:S(2)}) copy-start(f32[512]{0:T(512)S(1)} %broadcast_multiply_fusion.2) | copy-start | bytes 6148
  16.0 130.7 %copy-start.40 = (f32[512]{0:T(512)}, f32[512]{0:T(512)S(1)}, u32[]{:S(2)}) copy-start(f32[512]{0:T(512)S(1)} %fusion.36) | copy-start | bytes 6148
  59.9 86.8 %copy-start.35 = (f32[1,1024]{1,0:T(1,128)}, f32[1,1024]{1,0:T(1,128)S(1)}, u32[]{:S(2)}) copy-start(f32[1,1024]{1,0:T(1,128)S(1)} %get-tuple-element.186) | copy-start | bytes 12292
  60.0 202.5 %copy-start.37 = (f32[1,1024]{1,0:T(1,128)}, f32[1,1024]{1,0:T(1,128)S(1)}, u32[]{:S(2)}) copy-start(f32[1,1024]{1,0:T(1,128)S(1)} %get-tuple-element.185) | copy-start | bytes 12292
  96.9 49.9 %copy-start.46 = (f32[1,1024]{1,0:T(1,128)}, f32[1,1024]{1,0:T(1,128)S(1)}, u32[]{:S(2)}) copy-start(f32[1,1024]{1,0:T(1,128)S(1)} %get-tuple-element.189) | copy-start | bytes 12292
  96.9 165.6 %copy-start.48 = (f32[1,1024]{1,0:T(1,128)}, f32[1,1024]{1,0:T(1,128)S(1)}, u32[]{:S(2)}) copy-start(f32[1,1024]{1,0:T(1,128)S(1)} %get-tuple-element.188) | copy-start | bytes 12292
  96.9 302.6 %copy-start.44 = (f32[1,1024]{1,0:T(1,128)}, f32[1,1024]{1,0:T(1,128)S(1)}, u32[]{:S(2)}) copy-start(f32[1,1024]{1,0:T(1,128)S(1)} %get-tuple-element.187) | copy-start | bytes 12292
  172.0 8.4 copy-start.16
  207.8 59.3 %copy-start.29 = (f32[512]{0:T(512)}, f32[512]{0:T(512)S(1)}, u32[]{:S(2)}) copy-start(f32[512]{0:T(512)S(1)} %broadcast_multiply_fusion.1) | copy-start | bytes 6148
  209.4 57.6 %copy-start.33 = (f32[512]{0:T(512)}, f32[512]{0:T(512)S(1)}, u32[]{:S(2)}) copy-start(f32[512]{0:T(512)S(1)} %multiply_reduce_fusion.9) | copy-start | bytes 6148
  209.5 57.6 %copy-start.42 = (f32[512]{0:T(512)}, f32[512]{0:T(512)S(1)}, u32[]{:S(2)}) copy-start(f32[512]{0:T(512)S(1)} %fusion.37) | copy-start | bytes 6148
  262.5 6.9 copy-start.6
  399.5 78.9 %copy-start.39 = (f32[512]{0:T(512)S(1)}, f32[512]{0:T(512)}, u32[]{:S(2)}) copy-start(f32[512]{0:T(512)} %fusion.43) | copy-start | bytes 6148
  478.5 14.8 copy-start.12
  503.9 2.3 copy-start.55
  537.8 4.8 copy-start.1
  537.8 4.8 copy-start.15
  537.8 4.8 copy-start.30
  537.8 4.8 copy-start.38
  537.8 4.8 copy-start.43
  537.9 5.5 copy-start.54
  542.6 2.6 copy-start.19
  543.3 1.9 copy-start.34
  553.0 8.9 copy-start.9
  553.0 8.9 copy-start.17
  561.9 28.0 %copy-start.25 = (bf16[16,64,512]{2,1,0:T(8,128)(2,1)}, bf16[16,64,512]{2,1,0:T(8,128)(2,1)S(1)}, u32[]{:S(2)}) copy-start(bf16[16,64,512]{2,1,0:T(8,128)(2,1)S(1)} %fusion.24) | copy-start | bytes 3145732
  573.5 12.2 copy-start.8
  585.7 2.7 copy-start.7
  585.7 4.2 slice-start.2
  588.4 2.0 copy-start.3
  588.4 2.0 copy-start.28
  588.4 2.0 copy-start.36
  588.4 1.9 copy-start.41
  588.4 2.9 slice-start.3
  589.9 6.8 copy-start.18
  597.7 264.6 %reduce-scatter.30.cloned.1.call-start = ((), (), s32[]{:S(2)}) async-start(), calls=%async_computation.23 | async-start | bytes 540672
  598.9 403.3 %reduce-scatter.22.cloned.1.call-start = ((), (), s32[]{:S(2)}) async-start(), calls=%async_computation.19 | async-start | bytes 4325376 | tf_op jit(solution)/shard_map/reduce_scatter | solution.py:162
  604.1 537.8 %reduce-scatter.20.cloned.1.call-start = ((), (), s32[]{:S(2)}) async-start(), calls=%async_computation.18 | async-start | bytes 4325376 | tf_op jit(solution)/shard_map/reduce_scatter | solution.py:160
  610.3 671.2 %reduce-scatter.18.cloned.1.call-start = ((), (), s32[]{:S(2)}) async-start(), calls=%async_computation.17 | async-start | bytes 4325376 | tf_op jit(solution)/shard_map/reduce_scatter | solution.py:159
  614.8 814.1 %reduce-scatter.28.cloned.1.call-start = ((), (), s32[]{:S(2)}) async-start(), calls=%async_computation.22 | async-start | bytes 8650752
  615.0 7.1 copy-start.10
  622.1 10.0 copy-start.21
  649.4 937.2 %reduce-scatter.16.cloned.1.call-start = ((), (), s32[]{:S(2)}) async-start(), calls=%async_computation.16 | async-start | bytes 12976128 | tf_op jit(solution)/shard_map/reduce_scatter | solution.py:158
  660.9 1110.6 %reduce-scatter.24.cloned.1.call-start = ((), (), s32[]{:S(2)}) async-start(), calls=%async_computation.20 | async-start | bytes 17301504 | tf_op jit(solution)/shard_map/reduce_scatter | solution.py:163
  674.9 1283.8 %reduce-scatter.26.cloned.1.call-start = ((), (), s32[]{:S(2)}) async-start(), calls=%async_computation.21 | async-start | bytes 17301504 | tf_op jit(solution)/shard_map/reduce_scatter | solution.py:164
  689.0 4.7 copy-start.52
  692.1 1.6 copy-start.22
  692.1 2.6 copy-start.24
  692.1 7.0 slice-start
  694.7 4.5 copy-start.13
  694.7 4.5 slice-start.1
  694.7 4.6 copy-start.56
  (13 other events, 14.6 us)
Sparse Core Ops, SparseCore 0:
  10.9 64.9 all-gather.13
  78.7 67.9 all-gather.9
  149.6 54.8 all-gather.11
  207.2 55.2 all-gather.15
  265.2 55.2 all-gather.17
  323.2 76.2 all-gather.19
  402.4 76.0 all-gather.21
  597.9 132.5 reduce-scatter.31
  732.7 129.5 reduce-scatter.29
  865.1 137.1 reduce-scatter.21
  1005.1 136.7 reduce-scatter.19
  1144.6 136.7 reduce-scatter.17
  1284.3 144.5 reduce-scatter.27
  1435.4 151.2 reduce-scatter.15
  1589.5 181.9 reduce-scatter.23
  1774.3 184.3 reduce-scatter.25
where the time goes:
time: 1980 us; the launch traced here: 1970 us
  waiting for transfers between devices  1510 us (76%)
  matrix products  253 us (13%)
  blocking collectives  80 us (4%)
  other arithmetic  54.9 us (3%)
  local copies, waits for them, and re-layouts  54.1 us (3%)
    unnamed x19, waiting for transfers between devices  308 us
    reduce_scatter x1, waiting for transfers between devices, spread_grads(): lax.psum_scatter(gg, ('gx', 'gy'), scatter_dimension=0, tiled=True)  187 us
    reduce_scatter x1, waiting for transfers between devices, spread_grads(): lax.psum_scatter(gf, ('gx', 'gy'), scatter_dimension=0, tiled=True)  185 us
    reduce_scatter x1, waiting for transfers between devices, spread_grads(): lax.psum_scatter(ga, ('gx', 'gy'), scatter_dimension=0, tiled=True)  158 us
    reduce_scatter x1, waiting for transfers between devices, spread_grads(): lax.psum_scatter(gc, ('gx', 'gy'), scatter_dimension=0, tiled=True)  140 us
    reduce_scatter x1, waiting for transfers between devices, spread_grads(): lax.psum_scatter(gb, ('gx', 'gy'), scatter_dimension=0, tiled=True)  140 us
    reduce_scatter x1, waiting for transfers between devices, spread_grads(): lax.psum_scatter(ge, ('gx', 'gy'), scatter_dimension=0, tiled=True)  138 us
    all_gather x1, waiting for transfers between devices, collect_forward(): lax.all_gather(wf, ('gx', 'gy'), axis=0, tiled=True)  73.4 us
  transfers between devices with their start and end apart: 16, of which 15 were waited for; matrix products, arithmetic and copies ran while one was open for 12% of the time, Pallas kernels for 0%

commit v1 on v0

v1 whole, which is shorter than its diff:
```python
import functools

import jax
import jax.numpy as jnp
from jax import lax
from jax.experimental import pallas as pl
from jax.experimental.pallas import tpu as pltpu
from jax.sharding import PartitionSpec as P

HEADS = 16
MEM_BIG = 588
ALL = ("gx", "gy")
BF = jnp.bfloat16
F32 = jnp.float32
PAIR = 128


def dot(a, b):
    return jnp.dot(a, b, preferred_element_type=F32)


def dot_nt(a, b):
    return lax.dot_general(a, b, (((1,), (1,)), ((), ())), preferred_element_type=F32)


def dot_tn(a, b):
    return lax.dot_general(a, b, (((0,), (0,)), ((), ())), preferred_element_type=F32)


def allowed_t(key_count, q0, q1, limit, causal):
    key_at = lax.broadcasted_iota(jnp.int32, (key_count, q1 - q0), 0)
    ok = key_at < limit
    if causal:
        query_at = lax.broadcasted_iota(jnp.int32, (key_count, q1 - q0), 1) + q0
        ok = ok & (key_at <= query_at)
    return ok


def half_mask(width, half):
    lane = lax.broadcasted_iota(jnp.int32, (1, width), 1)
    return ((lane // (width // 2)) == half).astype(F32).astype(BF)


def attn_fwd_kernel(spans, causal, limit_ref, q_ref, k_ref, v_ref, o_ref, lse_ref):
    width = q_ref.shape[1]
    half = width // 2
    limit = limit_ref[0]
    scale = BF(half**-0.5)
    v_t = v_ref[...].T
    for q0, q1, keys in spans:
        query = q_ref[q0:q1, :] * scale
        ok = allowed_t(keys, q0, q1, limit, causal)
        outs = []
        for h in range(2):
            s = dot_nt(k_ref[:keys, :], query * half_mask(width, h))
            s = jnp.where(ok, s, -1e30)
            top = jnp.max(s, axis=0, keepdims=True)
            e = jnp.exp(s - top)
            total = jnp.sum(e, axis=0, keepdims=True)
            outs.append(dot(v_t[h * half : (h + 1) * half, :keys], e.astype(BF)) / total)
            lse_ref[0, h : h + 1, q0:q1] = top + jnp.log(total)
        o_ref[q0:q1, :] = jnp.concatenate(outs, axis=0).T.astype(BF)


def attn_bwd_kernel(
    spans, causal, limit_ref, q_ref, k_ref, v_ref, o_ref, do_ref, lse_ref, dq_ref, dk_ref, dv_ref
):
    width = q_ref.shape[1]
    half = width // 2
    limit = limit_ref[0]
    scale = BF(half**-0.5)
    k_t = k_ref[...].T * scale
    dk_ref_val = [None]
    total_k = k_ref.shape[0]
    dk = jnp.zeros((total_k, width), F32)
    dv = jnp.zeros((total_k, width), F32)
    del dk_ref_val
    for q0, q1, keys in spans:
        query = q_ref[q0:q1, :] * scale
        grad_o = do_ref[q0:q1, :]
        ok = allowed_t(keys, q0, q1, limit, causal)
        both = (grad_o.astype(F32) * o_ref[q0:q1, :].astype(F32)).T
        outs = []
        dk_part = jnp.zeros((keys, width), F32)
        dv_part = jnp.zeros((keys, width), F32)
        for h in range(2):
            mask = half_mask(width, h)
            query_h = query * mask
            grad_h = grad_o * mask
            inner = jnp.sum(both[h * half : (h + 1) * half], axis=0, keepdims=True)
            s = dot_nt(k_ref[:keys, :], query_h)
            p = jnp.where(ok, jnp.exp(s - lse_ref[0, h : h + 1, q0:q1]), 0.0)
            dv_part += dot(p.astype(BF), grad_h)
            dp = dot_nt(v_ref[:keys, :], grad_h)
            ds = (p * (dp - inner)).astype(BF)
            dk_part += dot(ds, query_h)
            outs.append(dot(k_t[h * half : (h + 1) * half, :keys], ds))
        dq_ref[q0:q1, :] = jnp.concatenate(outs, axis=0).T.astype(BF)
        if keys < total_k:
            pad = jnp.zeros((total_k - keys, width), F32)
            dk_part = jnp.concatenate([dk_part, pad], axis=0)
            dv_part = jnp.concatenate([dv_part, pad], axis=0)
        dk += dk_part
        dv += dv_part
    dk_ref[...] = dk.astype(BF)
    dv_ref[...] = dv.astype(BF)


def make_spans(queries, keys, causal):
    step = 256
    return tuple(
        (q, q + step, min(q + step, keys) if causal else keys) for q in range(0, queries, step)
    )


def attn_params():
    return pltpu.CompilerParams(
        dimension_semantics=("arbitrary",), vmem_limit_bytes=40 * 1024 * 1024
    )


def attn_fwd(q, kv, k_at, v_at, limit, causal):
    q_arr, q_at = q
    queries, keys = q_arr.shape[0], kv.shape[0]
    pairs = HEADS // 2
    return pl.pallas_call(
        functools.partial(attn_fwd_kernel, make_spans(queries, keys, causal), causal),
        grid_spec=pltpu.PrefetchScalarGridSpec(
            num_scalar_prefetch=1,
            grid=(pairs,),
            in_specs=[
                pl.BlockSpec((queries, PAIR), lambda p, _: (0, q_at + p)),
                pl.BlockSpec((keys, PAIR), lambda p, _: (0, k_at + p)),
                pl.BlockSpec((keys, PAIR), lambda p, _: (0, v_at + p)),
            ],
            out_specs=[
                pl.BlockSpec((queries, PAIR), lambda p, _: (0, p)),
                pl.BlockSpec((1, 2, queries), lambda p, _: (p, 0, 0)),
            ],
        ),
        out_shape=[
            jax.ShapeDtypeStruct((queries, pairs * PAIR), BF),
            jax.ShapeDtypeStruct((pairs, 2, queries), F32),
        ],
        compiler_params=attn_params(),
        cost_estimate=pl.CostEstimate(
            flops=16 * queries * keys * 256 * 4,
            bytes_accessed=8 * queries * 1024,
            transcendentals=16 * queries * keys,
        ),
        name="attn_fwd",
    )(limit, q_arr, kv, kv)


def attn_bwd(q, kv, k_at, v_at, o, do, lse, limit, causal):
    q_arr, q_at = q
    queries, keys = q_arr.shape[0], kv.shape[0]
    pairs = HEADS // 2
    q_block = pl.BlockSpec((queries, PAIR), lambda p, _: (0, p))
    k_block = pl.BlockSpec((keys, PAIR), lambda p, _: (0, p))
    return pl.pallas_call(
        functools.partial(attn_bwd_kernel, make_spans(queries, keys, causal), causal),
        grid_spec=pltpu.PrefetchScalarGridSpec(
            num_scalar_prefetch=1,
            grid=(pairs,),
            in_specs=[
                pl.BlockSpec((queries, PAIR), lambda p, _: (0, q_at + p)),
                pl.BlockSpec((keys, PAIR), lambda p, _: (0, k_at + p)),
                pl.BlockSpec((keys, PAIR), lambda p, _: (0, v_at + p)),
                q_block,
                q_block,
                pl.BlockSpec((1, 2, queries), lambda p, _: (p, 0, 0)),
            ],
            out_specs=[q_block, k_block, k_block],
        ),
        out_shape=[
            jax.ShapeDtypeStruct((queries, pairs * PAIR), BF),
            jax.ShapeDtypeStruct((keys, pairs * PAIR), BF),
            jax.ShapeDtypeStruct((keys, pairs * PAIR), BF),
        ],
        compiler_params=attn_params(),
        cost_estimate=pl.CostEstimate(
            flops=16 * queries * keys * 256 * 10,
            bytes_accessed=16 * queries * 1024,
            transcendentals=16 * queries * keys,
        ),
        name="attn_bwd",
    )(limit, q_arr, kv, kv, o, do, lse)


def norm_parts(v):
    center = v - jnp.mean(v, -1, keepdims=True)
    inverse = lax.rsqrt(jnp.mean(center * center, -1, keepdims=True) + 1e-05)
    return center * inverse, inverse


def norm_back(grad, unit, inverse, gain):
    gain_grad = jnp.sum(grad * unit, axis=0)
    bias_grad = jnp.sum(grad, axis=0)
    scaled = grad * gain
    mean_a = jnp.mean(scaled, -1, keepdims=True)
    mean_b = jnp.mean(scaled * unit, -1, keepdims=True)
    return inverse * (scaled - mean_a - unit * mean_b), gain_grad, bias_grad


def gather_rows(w):
    return lax.all_gather(w, ALL, axis=0, tiled=True)


def scatter_rows(g):
    part = lax.psum_scatter(g, "gy", scatter_dimension=0, tiled=True)
    return lax.psum_scatter(part, "gx", scatter_dimension=0, tiled=True)


def shards(
    hidden,
    memory,
    lengths,
    page_class,
    cotangent,
    w_self_qkv,
    w_self_out,
    w_cross_q,
    w_cross_kv,
    w_cross_out,
    w_fc1,
    w_fc2,
    norm_gains,
    norm_biases,
    *,
    nx,
    ny,
):
    n = nx * ny
    tokens, d = hidden.shape
    rows = w_fc1.shape[0]
    ff = w_fc1.shape[1]
    cuts = w_fc2.shape[0] // rows
    mem_rows = -(-memory.shape[0] // 16) * 16
    slots_used = jnp.where(page_class == 0, MEM_BIG, MEM_BIG // 4).astype(jnp.int32)

    norm_cols = jnp.concatenate([norm_gains, norm_biases], axis=0).T
    norm_cols = jnp.pad(norm_cols, ((0, 0), (0, 128 - norm_cols.shape[1])))
    first = jnp.concatenate([w_self_qkv, w_cross_kv, norm_cols], axis=1)
    second = jnp.concatenate([w_self_out, w_cross_q, w_cross_out], axis=1)
    up_local = (
        w_fc1.reshape(rows, nx, ny, cuts, rows).transpose(0, 3, 2, 1, 4).reshape(rows, ff)
    )
    down_local = jnp.concatenate(
        [w_fc2[c * rows : (c + 1) * rows] for c in range(cuts)], axis=1
    )
    w_first = gather_rows(first)
    w_second = gather_rows(second)
    wup = gather_rows(up_local)
    wdown = lax.all_gather(down_local, ("gy", "gx"), axis=0, tiled=True)

    wqkv = w_first[:, : 3 * d]
    wckv = w_first[:, 3 * d : 5 * d]
    norms = w_first[:, 5 * d : 5 * d + 6].T.astype(F32)
    gains, biases = norms[:3], norms[3:]
    wso, wcq, wco = w_second[:, :d], w_second[:, d : 2 * d], w_second[:, 2 * d :]

    place = jnp.arange(d)
    source = place % rows + ((place // rows) % nx * ny + place // (rows * nx)) * rows
    select = (source[:, None] == place[None, :]).astype(BF)

    def turned(a):
        return dot_nt(select, a).astype(BF)

    unit1, inv1 = norm_parts(hidden)
    h1 = (unit1 * gains[0] + biases[0]).astype(BF)
    qkv = dot(h1, wqkv).astype(BF)
    blocks = d // PAIR
    o, lse = attn_fwd((qkv, 0), qkv, blocks, 2 * blocks, lengths, True)
    x1 = hidden + dot(o, wso)
    unit2, inv2 = norm_parts(x1)
    h2 = (unit2 * gains[1] + biases[1]).astype(BF)
    qc = dot(h2, wcq).astype(BF)
    memory_pad = jnp.pad(memory, ((0, mem_rows - memory.shape[0]), (0, 0)))
    kvc = dot(memory_pad, wckv).astype(BF)
    o2, lse2 = attn_fwd((qc, 0), kvc, 0, blocks, slots_used, False)
    x2 = x1 + dot(o2, wco)
    unit3, inv3 = norm_parts(x2)
    h3 = (unit3 * gains[2] + biases[2]).astype(BF)
    u = dot(h3, wup)
    cdf = 0.5 * (1.0 + lax.erf(u * (0.5**0.5)))
    g = (u * cdf).astype(BF)
    slope = (cdf + u * (jnp.exp(-0.5 * u * u) * 0.3989422804014327)).astype(BF)
    result = x2
    for c in range(cuts):
        result = result + dot(g[:, c * d : (c + 1) * d], wdown[:, c * d : (c + 1) * d])

    valid = (jnp.arange(tokens) < lengths[0])[:, None].astype(F32)
    dout = cotangent * valid
    dy3 = dout.astype(BF)
    grad_down = jnp.concatenate(
        [dot_tn(g[:, c * d : (c + 1) * d], dy3).astype(BF) for c in range(cuts)], axis=1
    )
    own_down = scatter_rows(grad_down)
    dg = jnp.concatenate(
        [dot_nt(dy3, wdown[:, c * d : (c + 1) * d]) for c in range(cuts)], axis=1
    )
    du = (dg * slope.astype(F32)).astype(BF)
    grad_up = dot(turned(h3), du).astype(BF)
    own_up = scatter_rows(grad_up)
    dh3 = dot_nt(du, wup)
    back3, gain3, bias3 = norm_back(dh3, unit3, inv3, gains[2])
    dx2 = dout + back3
    dy2 = dx2.astype(BF)
    do2 = dot_nt(dy2, wco).astype(BF)
    dqc, dkc, dvc = attn_bwd((qc, 0), kvc, 0, blocks, o2, do2, lse2, slots_used, False)
    dkvc = jnp.concatenate([dkc, dvc], axis=1)
    mem_turned = turned(memory_pad)
    grad_mid = jnp.concatenate(
        [
            dot(turned(o2), dy2).astype(BF),
            dot(turned(h2), dqc).astype(BF),
            dot(mem_turned, dkvc).astype(BF),
        ],
        axis=1,
    )
    own_mid = scatter_rows(grad_mid)
    grad_memory = dot_nt(dkvc, wckv)[: memory.shape[0]]
    dh2 = dot_nt(dqc, wcq)
    back2, gain2, bias2 = norm_back(dh2, unit2, inv2, gains[1])
    dx1 = dx2 + back2
    dy1 = dx1.astype(BF)
    do = dot_nt(dy1, wso).astype(BF)
    dq, dk, dv = attn_bwd((qkv, 0), qkv, blocks, 2 * blocks, o, do, lse, lengths, True)
    dqkv = jnp.concatenate([dq, dk, dv], axis=1)
    dh1 = dot_nt(dqkv, wqkv)
    back1, gain1, bias1 = norm_back(dh1, unit1, inv1, gains[0])
    grad_hidden = dx1 + back1
    norm_grads = jnp.stack([gain1, gain2, gain3, bias1, bias2, bias3])
    norm_grads = jnp.pad(norm_grads, ((0, 122), (0, 0))).astype(BF)
    grad_last = jnp.concatenate(
        [
            dot(turned(o), dy1).astype(BF),
            dot(turned(h1), dqkv).astype(BF),
            turned(norm_grads),
        ],
        axis=1,
    )
    own_last = scatter_rows(grad_last)

    own_up = (
        own_up.reshape(rows, cuts, ny, nx, rows).transpose(0, 3, 2, 1, 4).reshape(rows, ff)
    )
    own_down = jnp.concatenate(
        [own_down[:, c * d : (c + 1) * d] for c in range(cuts)], axis=0
    )
    own_norms = own_last[:, 4 * d : 4 * d + 6].T.astype(F32)
    return (
        result,
        grad_hidden,
        grad_memory,
        own_last[:, d : 4 * d].astype(F32),
        own_last[:, :d].astype(F32),
        own_mid[:, d : 2 * d].astype(F32),
        own_mid[:, 2 * d :].astype(F32),
        own_mid[:, :d].astype(F32),
        own_up.astype(F32),
        own_down.astype(F32),
        own_norms[:3],
        own_norms[3:],
    )


def solution(mesh):
    row = P(ALL, None)
    col = P(None, ALL)
    return jax.shard_map(
        functools.partial(shards, nx=mesh.shape["gx"], ny=mesh.shape["gy"]),
        mesh=mesh,
        in_specs=(row, row, P(ALL), P(ALL), row) + (row,) * 7 + (col, col),
        out_specs=(row,) * 10 + (col, col),
        check_vma=False,
    )
```

time: 1980 us -> 789 us (0.40)
  waiting for transfers between devices: 1510 us -> 464 us
  matrix products: 253 us -> 143 us
  blocking collectives: 80 us -> 0 us
  Pallas kernels: 0 us -> 63.1 us
    reduce_scatter x6, waiting for transfers between devices: 947 us -> 200 us  [the longest x3 132 us: scatter_rows(): part = lax.psum_scatter(g, 'gy', scatter_dimension=0, tiled=True)]
    unnamed x19 -> x14, waiting for transfers between devices: 308 us -> 19.9 us
    dot_general x33 -> x31, matrix products: 253 us -> 143 us  [the longest x16 88.9 us: dot(): return jnp.dot(a, b, preferred_element_type=F32)]
    all_gather x2 -> x0, blocking collectives: 80 us -> none  [the longest x1 43.2 us: collect_forward(): lax.all_gather(gain_rows, ('gx', 'gy'), axis=1, tiled=True)]
    pallas_call x0 -> x4, Pallas kernels: none -> 63.1 us  [the longest x2 31.9 us: attn_bwd(): pl.pallas_call(functools.partial(attn_bwd_kernel, make_spans(queries, key...]
    reduce_sum x9 -> x4, other arithmetic: 24.9 us -> 1.22 us  [the longest x3 1.04 us: norm_parts(): inverse = lax.rsqrt(jnp.mean(center * center, -1, keepdims=True) + 1e-05)]
    concatenate x0 -> x6, other arithmetic: none -> 21.4 us  [the longest x1 7.08 us: shards(): jnp.concatenate([dot(turned(o), dy1).astype(BF), dot(turned(h1), dqkv).as...]
    all_gather x7 -> x4, waiting for transfers between devices: 251 us -> 243 us  [the longest x3 173 us: gather_rows(): return lax.all_gather(w, ALL, axis=0, tiled=True)]
  transfers between devices with their start and end apart: 16 -> 12, of which waited for: 15 -> 10; matrix products, arithmetic and copies ran while one was open for 12% -> 25% of each run, Pallas kernels for 0% -> 8%
where the time goes in v1:
time: 789 us; the launch traced here: 781 us
  waiting for transfers between devices  464 us (59%)
  matrix products  143 us (18%)
  Pallas kernels  63.1 us (8%)
  local copies, waits for them, and re-layouts  56.5 us (7%)
  other arithmetic  37.7 us (5%)
  between operations  16.9 us (2%)
    all_gather x3, waiting for transfers between devices, gather_rows(): return lax.all_gather(w, ALL, axis=0, tiled=True)  173 us
    reduce_scatter x3, waiting for transfers between devices, scatter_rows(): part = lax.psum_scatter(g, 'gy', scatter_dimension=0, tiled=True)  132 us
    dot_general x16, matrix products, dot(): return jnp.dot(a, b, preferred_element_type=F32)  88.9 us
    all_gather x1, waiting for transfers between devices, shards(): wdown = lax.all_gather(down_local, ('gy', 'gx'), axis=0, tiled=True)  70.3 us
    reduce_scatter x3, waiting for transfers between devices, scatter_rows(): return lax.psum_scatter(part, 'gx', scatter_dimension=0, tiled=True)  68.7 us
    dot_general x11, matrix products, dot_nt(): lax.dot_general(a, b, (((1,), (1,)), ((), ())), preferred_element_type=F32)  46.9 us
    pallas_call x2, Pallas kernels, attn_bwd(): pl.pallas_call(functools.partial(attn_bwd_kernel, make_spans(queries, key...  31.9 us
    pallas_call x2, Pallas kernels, attn_fwd(): pl.pallas_call(functools.partial(attn_fwd_kernel, make_spans(queries, key...  31.2 us
  transfers between devices with their start and end apart: 12, of which 10 were waited for; matrix products, arithmetic and copies ran while one was open for 25% of the time, Pallas kernels for 8%

profile of v1, /device:TPU:0, one launch (start us, length us, event | category | flops | bytes accessed | tf_op | source)
XLA Modules:
  0.0 781.2 jit_solution(17261991970905773202)
XLA Ops:
  9.9 1.7 fusion.104
  12.5 1.8 reshape.145
  14.3 1.9 copy.66
  16.2 1.8 reshape.146
  21.4 70.3 %all-gather.11.cloned.1.call-done = bf16[1024,4096]{1,0:T(8,128)(2,1)} async-done(((bf16[32,4096]{1,0:T(8,128)(2,1)}), bf16[1024,4096]{1,0:T(8,128)(2,1)}) %all-gather.11.cloned.1.call-update) | async-done | bytes 8388624 | tf_op jit(solution)/shard_map/all_gather | solution.py:255
  91.7 4.3 fusion.35
  96.0 2.6 fusion.39
  98.6 2.7 fusion.43
  101.3 2.6 fusion.47
  103.9 77.5 %all-gather.5.cloned.1.call-done = bf16[1024,5248]{1,0:T(8,128)(2,1)} async-done(((bf16[32,5248]{1,0:T(8,128)(2,1)}), bf16[1024,5248]{1,0:T(8,128)(2,1)}) %all-gather.5.cloned.1.call-update) | async-done | bytes 10747920 | tf_op jit(solution)/shard_map/all_gather | solution.py:207
  182.4 1.6 slice_reduce_fusion.1
  184.6 6.8 fusion.10.q_ref.k_ref.v_ref
  191.4 13.6 %attn_fwd.2 = (bf16[512,1024]{1,0:T(8,128)(2,1)S(1)}, f32[8,2,512]{2,1,0:T(2,128)S(1)}) custom-call(s32[1]{0:T(128)} %copy.70.limit_ref, bf16[512,3072]{1,0:T(8,128)(2,1)S(1)} %fusion.10.q_ref.k_ref.v_ref, bf16[512,3072]{1,0:T(8,128)(2,1)S(1)} %fusion.10.q_ref.k_ref.v_ref, bf16[512,3072]{1,0:T(8,128)(2,1)S(1)} %fusion.10.q_ref.k_ref.v_ref), custom_call_target="tpu_custom_call" | custom-call | flops 4294967296 | bytes 4194304 | tf_op jit(solution)/shard_map/attn_fwd/pallas_call | solution.py:126
  205.0 1.6 copy-done.4
  206.6 46.3 %all-gather.7.cloned.1.call-done = bf16[1024,3072]{1,0:T(8,128)(2,1)} async-done(((bf16[32,3072]{1,0:T(8,128)(2,1)}), bf16[1024,3072]{1,0:T(8,128)(2,1)}) %all-gather.7.cloned.1.call-update) | async-done | bytes 6291472 | tf_op jit(solution)/shard_map/all_gather | solution.py:207
  252.9 3.1 fusion.129
  256.5 1.3 fusion.73.q_ref
  258.1 5.5 fusion.24.k_ref.v_ref
  263.6 17.6 %attn_fwd.3 = (bf16[512,1024]{1,0:T(8,128)(2,1)S(1)}, f32[8,2,512]{2,1,0:T(2,128)S(1)}) custom-call(s32[1]{0:T(128)S(6)} %select_n.87.limit_ref, bf16[512,1024]{1,0:T(8,128)(2,1)S(1)} %fusion.73.q_ref, bf16[592,2048]{1,0:T(8,128)(2,1)S(1)} %fusion.24.k_ref.v_ref, bf16[592,2048]{1,0:T(8,128)(2,1)S(1)} %fusion.24.k_ref.v_ref), custom_call_target="tpu_custom_call" | custom-call | flops 4966055936 | bytes 4194304 | tf_op jit(solution)/shard_map/attn_fwd/pallas_call | solution.py:126
  281.3 1.4 fusion.130
  283.0 49.2 %all-gather.9.cloned.1.call-done = bf16[1024,4096]{1,0:T(8,128)(2,1)} async-done(((bf16[32,4096]{1,0:T(8,128)(2,1)}), bf16[1024,4096]{1,0:T(8,128)(2,1)}) %all-gather.9.cloned.1.call-update) | async-done | bytes 8388624 | tf_op jit(solution)/shard_map/all_gather | solution.py:207
  332.2 15.0 %fusion.5 = (bf16[512,4096]{1,0:T(8,128)(2,1)}, bf16[512,4096]{1,0:T(8,128)(2,1)}) fusion(f32[512,1024]{1,0:T(8,128)} %fusion.35, f32[512,1024]{1,0:T(8,128)} %fusion.39, f32[512,1024]{1,0:T(8,128)} %fusion.43, f32[512,1024]{1,0:T(8,128)} %fusion.47, bf16[1024,4096]{1,0:T(8,128)(2,1)} %all-gather.9.cloned.1.call-done, ...), kind=kOutput, calls=%fused_computation.8 | convolution fusion | flops 4333240320 | bytes 27275264 | tf_op jit(solution)/shard_map/dot_general | solution.py:19
  347.2 10.7 %convolution_convert_fusion = bf16[1024,4096]{1,0:T(8,128)(2,1)} fusion(bf16[512,4096]{1,0:T(8,128)(2,1)} %get-tuple-element.86, s32[1024]{0:T(1024)S(1)} %fusion.116, f32[512,1024]{1,0:T(8,128)S(1)} %get-tuple-element.103, f32[1024]{0:T(1024)S(1)} %get-tuple-element.81, f32[1024]{0:T(1024)S(1)} %get-tuple-element.80, f32[512]{0:T(512)S(1)} %add_rsqrt_fusion, ...), kind=kOutput, calls=%fused_computation.13 | convolution fusion | flops 5377097728 | bytes 14696448 | tf_op jit(solution)/shard_map/dot_general | solution.py:19
  358.0 3.0 convolution_convert_fusion.3
  362.5 1.3 convolution_convert_fusion.5
  363.8 1.3 convolution_convert_fusion.6
  365.1 4.6 pad_maximum_fusion.2
  369.7 12.3 %copy.56 = bf16[1024,4096]{1,0:T(8,128)(2,1)} copy(bf16[1024,4096]{0,1:T(8,128)(2,1)} %pad_maximum_fusion.2) | data formatting | bytes 16777216
  382.0 10.0 %multiply_reduce_fusion = (bf16[1024]{0:T(1024)(128)(2,1)}, f32[512]{0:T(512)S(1)}, f32[512]{0:T(512)S(1)}, bf16[1024]{0:T(1024)(128)(2,1)}, f32[512,1024]{1,0:T(8,128)S(1)}) fusion(f32[512,1024]{1,0:T(8,128)S(1)} %get-tuple-element.103, f32[512]{0:T(512)S(1)} %add_rsqrt_fusion, f32[512]{0:T(512)S(1)} %broadcast_multiply_fusion.6, ...), kind=kOutput, calls=%fused_computation.35 | convolution fusion | flops 4299682816 | bytes 16793600 | tf_op jit(solution)/shard_map/dot_general | solution.py:23
  392.9 3.7 fusion.76.do_ref
  396.7 18.0 %attn_bwd.2 = (bf16[512,1024]{1,0:T(8,128)(2,1)S(1)}, bf16[592,1024]{1,0:T(8,128)(2,1)S(1)}, bf16[592,1024]{1,0:T(8,128)(2,1)S(1)}) custom-call(s32[1]{0:T(128)S(6)} %select_n.87.limit_ref, bf16[512,1024]{1,0:T(8,128)(2,1)S(1)} %copy-done.9, bf16[592,2048]{1,0:T(8,128)(2,1)S(1)} %copy-done.7, bf16[592,2048]{1,0:T(8,128)(2,1)S(1)} %copy-done.7, ...), custom_call_target="tpu_custom_call" | custom-call | flops 12415139840 | bytes 8388608 | tf_op jit(solution)/shard_map/attn_bwd/pallas_call | solution.py:161
  415.6 5.7 convolution_convert_fusion.7
  421.4 4.0 copy.50
  425.3 5.6 convolution_convert_fusion.8
  430.9 4.1 copy.49
  437.4 9.4 %convolution_convert_fusion.2 = bf16[1024,2048]{1,0:T(8,128)(2,1)} fusion(bf16[592,2048]{1,0:T(8,128)(2,1)} %constant_dynamic-update-slice_fusion.3, s32[1024]{0:T(1024)S(1)} %copy-done.41, bf16[588,1024]{1,0:T(8,128)(2,1)} %param.15), kind=kOutput, calls=%fused_computation.28 | convolution fusion | flops 3728293888 | bytes 7827456 | tf_op jit(solution)/shard_map/dot_general | solution.py:19
  446.7 6.6 pad_maximum_fusion.1
  454.6 4.3 multiply_reduce_fusion.1
  459.7 3.7 fusion.70.do_ref
  463.4 13.9 %attn_bwd.3 = (bf16[512,1024]{1,0:T(8,128)(2,1)S(1)}, bf16[512,1024]{1,0:T(8,128)(2,1)S(1)}, bf16[512,1024]{1,0:T(8,128)(2,1)S(1)}) custom-call(s32[1]{0:T(128)} %copy.70.limit_ref, bf16[512,3072]{1,0:T(8,128)(2,1)S(1)} %copy-done.5, bf16[512,3072]{1,0:T(8,128)(2,1)S(1)} %copy-done.5, bf16[512,3072]{1,0:T(8,128)(2,1)S(1)} %copy-done.5, ...), custom_call_target="tpu_custom_call" | custom-call | flops 10737418240 | bytes 8388608 | tf_op jit(solution)/shard_map/attn_bwd/pallas_call | solution.py:161
  477.6 1.4 copy-done.11
  479.0 5.1 multiply_reduce_fusion.2
  484.2 5.3 convolution_convert_fusion.9
  489.5 4.0 copy.48
  494.3 8.8 %convolution_convert_fusion.1 = bf16[1024,3072]{1,0:T(8,128)(2,1)} fusion(bf16[512,3072]{1,0:T(8,128)(2,1)} %copy-done.25, s32[1024]{0:T(1024)S(1)} %copy-done.41, f32[512,1024]{1,0:T(8,128)S(1)} %copy-done.11, f32[1024]{0:T(1024)S(1)} %copy-done.39, f32[1024]{0:T(1024)S(1)} %copy-done.35, f32[512]{0:T(512)S(1)} %copy-done.37, f32[512]{0:T(512)S(1)} %copy-done.33), kind=kOutput, calls=%fused_computation.14 | convolution fusion | flops 4302307328 | bytes 11550720 | tf_op jit(solution)/shard_map/dot_general | solution.py:19
  503.1 7.1 pad_maximum_fusion
  511.6 66.1 %reduce-scatter.17.cloned.1.call-done = bf16[128,4096]{1,0:T(8,128)(2,1)} async-done(((bf16[1024,4096]{1,0:T(8,128)(2,1)}), bf16[128,4096]{1,0:T(8,128)(2,1)}) %reduce-scatter.17.cloned.1.call-update) | async-done | bytes 1048592 | tf_op jit(solution)/shard_map/reduce_scatter | solution.py:211
  578.1 3.3 fusion.37
  581.4 3.0 fusion.41
  586.1 2.7 add_add_fusion
  588.8 65.5 %reduce-scatter.13.cloned.1.call-done = bf16[128,4224]{1,0:T(8,128)(2,1)} async-done(((bf16[1024,4224]{1,0:T(8,128)(2,1)}), bf16[128,4224]{1,0:T(8,128)(2,1)}) %reduce-scatter.13.cloned.1.call-update) | async-done | bytes 1081360 | tf_op jit(solution)/shard_map/reduce_scatter | solution.py:211
  654.4 4.2 multiply_add_fusion
  658.6 7.0 fusion.20
  665.6 18.2 %reduce-scatter.23.cloned.1.call-done = bf16[32,4096]{1,0:T(8,128)(2,1)} async-done(((bf16[128,4096]{1,0:T(8,128)(2,1)}), bf16[32,4096]{1,0:T(8,128)(2,1)}) %reduce-scatter.23.cloned.1.call-update) | async-done | bytes 262160 | tf_op jit(solution)/shard_map/reduce_scatter | solution.py:212
  683.8 3.4 reshape.148
  687.2 3.4 copy.51
  690.6 2.7 reshape.147
  693.3 18.6 %reduce-scatter.27.cloned.1.call-done = bf16[32,4096]{1,0:T(8,128)(2,1)} async-done(((bf16[128,4096]{1,0:T(8,128)(2,1)}), bf16[32,4096]{1,0:T(8,128)(2,1)}) %reduce-scatter.27.cloned.1.call-update) | async-done | bytes 262160
  714.9 25.1 %reduce-scatter.19.cloned.1.call-done = bf16[32,4096]{1,0:T(8,128)(2,1)} async-done(((bf16[128,4096]{1,0:T(8,128)(2,1)}), bf16[32,4096]{1,0:T(8,128)(2,1)}) %reduce-scatter.19.cloned.1.call-update) | async-done | bytes 262160 | tf_op jit(solution)/shard_map/reduce_scatter | solution.py:212
  740.0 1.6 slice_convert_fusion.2
  741.6 1.6 slice_convert_fusion.1
  743.2 25.4 %reduce-scatter.15.cloned.1.call-done = bf16[32,4224]{1,0:T(8,128)(2,1)} async-done(((bf16[128,4224]{1,0:T(8,128)(2,1)}), bf16[32,4224]{1,0:T(8,128)(2,1)}) %reduce-scatter.15.cloned.1.call-update) | async-done | bytes 270352 | tf_op jit(solution)/shard_map/reduce_scatter | solution.py:212
  770.7 1.7 slice_convert_fusion
  772.4 1.5 slice_convert_fusion.4
  (183 shorter events, 25.3 us)
Async XLA Ops:
  7.2 4.5 copy-start.29
  7.2 4.5 copy-start.30
  7.2 4.5 copy-start.31
  7.2 5.3 copy-start.26
  7.2 84.5 %all-gather.11.cloned.1.call-start = ((), (), s32[]{:S(2)}) async-start(), calls=%async_computation.11 | async-start | bytes 8650752 | tf_op jit(solution)/shard_map/all_gather | solution.py:255
  9.0 172.4 %all-gather.5.cloned.1.call-start = ((), (), s32[]{:S(2)}) async-start(), calls=%async_computation.8 | async-start | bytes 11083776 | tf_op jit(solution)/shard_map/all_gather | solution.py:207
  11.7 241.3 %all-gather.7.cloned.1.call-start = ((), (), s32[]{:S(2)}) async-start(), calls=%async_computation.9 | async-start | bytes 6488064 | tf_op jit(solution)/shard_map/all_gather | solution.py:207
  12.5 319.8 %all-gather.9.cloned.1.call-start = ((), (), s32[]{:S(2)}) async-start(), calls=%async_computation.10 | async-start | bytes 8650752 | tf_op jit(solution)/shard_map/all_gather | solution.py:207
  14.3 5.1 copy-start.10
  18.1 492.2 %reduce-scatter.21.cloned.1.call-start = ((), (), s32[]{:S(2)}) async-start(), calls=%async_computation.16 | async-start | bytes 9437184 | tf_op jit(solution)/shard_map/reduce_scatter | solution.py:211
  19.6 1.6 copy-start.17
  19.6 327.6 %copy-start.40 = (s32[1024]{0:T(1024)}, s32[1024]{0:T(1024)S(1)}, u32[]{:S(2)}) copy-start(s32[1024]{0:T(1024)S(1)} %fusion.116) | copy-start | bytes 12292
  19.7 164.4 %copy-start.32 = (f32[512]{0:T(512)}, f32[512]{0:T(512)S(1)}, u32[]{:S(2)}) copy-start(f32[512]{0:T(512)S(1)} %broadcast_multiply_fusion.8) | copy-start | bytes 6148
  21.2 162.8 %copy-start.36 = (f32[512]{0:T(512)}, f32[512]{0:T(512)S(1)}, u32[]{:S(2)}) copy-start(f32[512]{0:T(512)S(1)} %add_rsqrt_fusion.2) | copy-start | bytes 6148
  21.4 80.0 %copy-start.22 = (bf16[512,1024]{1,0:T(8,128)(2,1)}, bf16[512,1024]{1,0:T(8,128)(2,1)S(1)}, u32[]{:S(2)}) copy-start(bf16[512,1024]{1,0:T(8,128)(2,1)S(1)} %multiply_convert_fusion.1) | copy-start | bytes 3145732
  91.7 4.4 copy-start.24
  184.0 0.6 copy-start.38
  184.0 7.4 copy-start.34
  205.0 1.6 copy-start.4
  252.9 3.5 slice-start.5
  252.9 3.5 slice-start.6
  256.0 25.3 %copy-start.19 = (f32[512,1024]{1,0:T(8,128)}, f32[512,1024]{1,0:T(8,128)S(1)}, u32[]{:S(2)}) copy-start(f32[512,1024]{1,0:T(8,128)S(1)} %get-tuple-element.101) | copy-start | bytes 6291460
  256.5 1.6 copy-start.44
  258.1 5.6 copy-start.8
  263.6 17.7 %copy-start.6 = (bf16[592,2048]{1,0:T(8,128)(2,1)}, bf16[592,2048]{1,0:T(8,128)(2,1)S(1)}, u32[]{:S(2)}) copy-start(bf16[592,2048]{1,0:T(8,128)(2,1)S(1)} %fusion.24.k_ref.v_ref) | copy-start | bytes 7274500
  281.3 1.4 copy-start
  282.7 109.4 %copy-start.12 = (f32[512,1024]{1,0:T(8,128)}, f32[512,1024]{1,0:T(8,128)S(1)}, u32[]{:S(2)}) copy-start(f32[512,1024]{1,0:T(8,128)S(1)} %get-tuple-element.103) | copy-start | bytes 6291460
  358.0 153.1 %reduce-scatter.25.cloned.1.call-start = ((), (), s32[]{:S(2)}) async-start(), calls=%async_computation.18 | async-start | bytes 9437184
  358.0 3.0 copy-start.23
  358.0 3.1 copy-start.27
  382.0 195.7 %reduce-scatter.17.cloned.1.call-start = ((), (), s32[]{:S(2)}) async-start(), calls=%async_computation.14 | async-start | bytes 9437184 | tf_op jit(solution)/shard_map/reduce_scatter | solution.py:211
  382.0 10.0 %copy-start.18 = (f32[512,1024]{1,0:T(8,128)S(1)}, f32[512,1024]{1,0:T(8,128)}, u32[]{:S(2)}) copy-start(f32[512,1024]{1,0:T(8,128)} %param.18) | copy-start | bytes 6291460
  392.9 3.8 copy-start.15
  392.9 3.8 copy-start.1
  392.9 3.8 copy-start.7
  392.9 3.8 copy-start.9
  414.7 1.0 copy-start.2
  421.4 4.0 copy-start.41
  437.4 9.4 %copy-start.21 = (bf16[1024,1024]{1,0:T(8,128)(2,1)S(1)}, bf16[1024,1024]{1,0:T(8,128)(2,1)}, u32[]{:S(2)}) copy-start(bf16[1024,1024]{1,0:T(8,128)(2,1)} %copy.50) | copy-start | bytes 6291460
  453.3 1.2 copy-start.3
  453.4 201.0 %reduce-scatter.13.cloned.1.call-start = ((), (), s32[]{:S(2)}) async-start(), calls=%async_computation.12 | async-start | bytes 9732096 | tf_op jit(solution)/shard_map/reduce_scatter | solution.py:211
  454.6 4.3 copy-start.16
  454.6 4.3 copy-start.20
  459.6 3.7 copy-start.14
  459.6 3.7 copy-start.5
  459.6 17.9 %slice-start.2 = ((s8[10747904]{0:T(1024)(128)(4,1)}), s8[4194304]{0:T(1024)(128)(4,1)S(1)}, s32[]{:S(2)}) async-start(s8[10747904]{0:T(1024)(128)(4,1)} %bitcast.39), calls=%async_computation.22 | async-start | bytes 8388608
  463.3 14.2 %slice-start.3 = ((s8[10747904]{0:T(1024)(128)(4,1)}), s8[4194304]{0:T(1024)(128)(4,1)S(1)}, s32[]{:S(2)}) async-start(s8[10747904]{0:T(1024)(128)(4,1)} %bitcast.39), calls=%async_computation.23 | async-start | bytes 8388608
  463.4 14.2 %slice-start.4 = ((s8[10747904]{0:T(1024)(128)(4,1)}), s8[2359296]{0:T(1024)(128)(4,1)S(1)}, s32[]{:S(2)}) async-start(s8[10747904]{0:T(1024)(128)(4,1)} %bitcast.39), calls=%async_computation.24 | async-start | bytes 4718592
  477.4 1.6 copy-start.11
  477.4 1.6 copy-start.33
  477.4 1.6 copy-start.35
  477.4 1.6 copy-start.37
  479.0 5.1 copy-start.25
  479.0 5.1 copy-start.43
  479.0 5.2 copy-start.42
  493.4 0.9 copy-start.39
  510.2 173.6 %reduce-scatter.23.cloned.1.call-start = ((), (), s32[]{:S(2)}) async-start(), calls=%async_computation.17 | async-start | bytes 1310720 | tf_op jit(solution)/shard_map/reduce_scatter | solution.py:212
  511.0 200.9 %reduce-scatter.27.cloned.1.call-start = ((), (), s32[]{:S(2)}) async-start(), calls=%async_computation.19 | async-start | bytes 1310720
  511.6 228.4 %reduce-scatter.19.cloned.1.call-start = ((), (), s32[]{:S(2)}) async-start(), calls=%async_computation.15 | async-start | bytes 1310720 | tf_op jit(solution)/shard_map/reduce_scatter | solution.py:212
  577.7 190.9 %reduce-scatter.15.cloned.1.call-start = ((), (), s32[]{:S(2)}) async-start(), calls=%async_computation.13 | async-start | bytes 1351680 | tf_op jit(solution)/shard_map/reduce_scatter | solution.py:212
  578.1 3.3 copy-start.28
  578.1 6.3 slice-start
  581.4 3.1 slice-start.1
  584.6 1.6 copy-start.13
Sparse Core Ops, SparseCore 0:
  11.6 80.0 all-gather.10
  95.1 86.2 all-gather.4
  184.9 68.0 all-gather.6
  256.2 75.9 all-gather.8
  358.1 69.8 reduce-scatter.20
  431.7 71.2 reduce-scatter.24
  506.4 71.2 reduce-scatter.16
  581.7 72.6 reduce-scatter.12
  656.6 27.1 reduce-scatter.22
  686.0 25.7 reduce-scatter.26
  714.2 25.7 reduce-scatter.18
  742.3 26.3 reduce-scatter.14

commit v2 on v1

--- a/solution.py
+++ b/solution.py
@@ -25,6 +25,41 @@
 
 def dot_tn(a, b):
     return lax.dot_general(a, b, (((0,), (0,)), ((), ())), preferred_element_type=F32)
+
+
+def run(kernel, grid, ins, outs, prefetch=(), scratch=(), deps=(), cost=None, name=None):
+    count = len(prefetch) + len(ins)
+
+    def body(*refs):
+        return kernel(*refs[:count], *refs[count + len(deps) :])
+
+    result = pl.pallas_call(
+        body,
+        grid_spec=pltpu.PrefetchScalarGridSpec(
+            num_scalar_prefetch=len(prefetch),
+            grid=grid,
+            in_specs=[spec for _, spec in ins] + [pl.BlockSpec(memory_space=pl.ANY)] * len(deps),
+            out_specs=[spec for _, spec in outs],
+            scratch_shapes=scratch,
+        ),
+        out_shape=[shape for shape, _ in outs],
+        compiler_params=pltpu.CompilerParams(
+            dimension_semantics=("arbitrary",) * len(grid), vmem_limit_bytes=48 * 1024 * 1024
+        ),
+        cost_estimate=cost,
+        name=name,
+    )(*prefetch, *[a for a, _ in ins], *deps)
+    return result if len(outs) > 1 else result[0]
+
+
+def costs(flops, nbytes, transcendentals=0):
+    return pl.CostEstimate(
+        flops=flops, bytes_accessed=nbytes, transcendentals=transcendentals
+    )
+
+
+def shaped(shape, dtype):
+    return jax.ShapeDtypeStruct(shape, dtype)
 
 
 def allowed_t(key_count, q0, q1, limit, causal):
@@ -70,11 +105,9 @@
     limit = limit_ref[0]
     scale = BF(half**-0.5)
     k_t = k_ref[...].T * scale
-    dk_ref_val = [None]
     total_k = k_ref.shape[0]
     dk = jnp.zeros((total_k, width), F32)
     dv = jnp.zeros((total_k, width), F32)
-    del dk_ref_val
     for q0, q1, keys in spans:
         query = q_ref[q0:q1, :] * scale
         grad_o = do_ref[q0:q1, :]
@@ -113,79 +146,62 @@
     )
 
 
-def attn_params():
-    return pltpu.CompilerParams(
-        dimension_semantics=("arbitrary",), vmem_limit_bytes=40 * 1024 * 1024
-    )
-
-
-def attn_fwd(q, kv, k_at, v_at, limit, causal):
+def attn_fwd(q, kv, k_at, v_at, limit, causal, deps=()):
     q_arr, q_at = q
     queries, keys = q_arr.shape[0], kv.shape[0]
     pairs = HEADS // 2
-    return pl.pallas_call(
+    return run(
         functools.partial(attn_fwd_kernel, make_spans(queries, keys, causal), causal),
-        grid_spec=pltpu.PrefetchScalarGridSpec(
-            num_scalar_prefetch=1,
-            grid=(pairs,),
-            in_specs=[
-                pl.BlockSpec((queries, PAIR), lambda p, _: (0, q_at + p)),
-                pl.BlockSpec((keys, PAIR), lambda p, _: (0, k_at + p)),
-                pl.BlockSpec((keys, PAIR), lambda p, _: (0, v_at + p)),
-            ],
-            out_specs=[
+        (pairs,),
+        [
+            (q_arr, pl.BlockSpec((queries, PAIR), lambda p, _: (0, q_at + p))),
+            (kv, pl.BlockSpec((keys, PAIR), lambda p, _: (0, k_at + p))),
+            (kv, pl.BlockSpec((keys, PAIR), lambda p, _: (0, v_at + p))),
+        ],
+        [
+            (
+                shaped((queries, pairs * PAIR), BF),
                 pl.BlockSpec((queries, PAIR), lambda p, _: (0, p)),
+            ),
+            (
+                shaped((pairs, 2, queries), F32),
                 pl.BlockSpec((1, 2, queries), lambda p, _: (p, 0, 0)),
-            ],
-        ),
-        out_shape=[
-            jax.ShapeDtypeStruct((queries, pairs * PAIR), BF),
-            jax.ShapeDtypeStruct((pairs, 2, queries), F32),
-        ],
-        compiler_params=attn_params(),
-        cost_estimate=pl.CostEstimate(
-            flops=16 * queries * keys * 256 * 4,
-            bytes_accessed=8 * queries * 1024,
-            transcendentals=16 * queries * keys,
-        ),
+            ),
+        ],
+        prefetch=(limit,),
+        deps=deps,
+        cost=costs(16 * queries * keys * 1024, 8 * queries * 1024, 16 * queries * keys),
         name="attn_fwd",
-    )(limit, q_arr, kv, kv)
-
-
-def attn_bwd(q, kv, k_at, v_at, o, do, lse, limit, causal):
+    )
+
+
+def attn_bwd(q, kv, k_at, v_at, o, do, lse, limit, causal, deps=()):
     q_arr, q_at = q
     queries, keys = q_arr.shape[0], kv.shape[0]
     pairs = HEADS // 2
     q_block = pl.BlockSpec((queries, PAIR), lambda p, _: (0, p))
     k_block = pl.BlockSpec((keys, PAIR), lambda p, _: (0, p))
-    return pl.pallas_call(
+    return run(
         functools.partial(attn_bwd_kernel, make_spans(queries, keys, causal), causal),
-        grid_spec=pltpu.PrefetchScalarGridSpec(
-            num_scalar_prefetch=1,
-            grid=(pairs,),
-            in_specs=[
-                pl.BlockSpec((queries, PAIR), lambda p, _: (0, q_at + p)),
-                pl.BlockSpec((keys, PAIR), lambda p, _: (0, k_at + p)),
-                pl.BlockSpec((keys, PAIR), lambda p, _: (0, v_at + p)),
-                q_block,
-                q_block,
-                pl.BlockSpec((1, 2, queries), lambda p, _: (p, 0, 0)),
-            ],
-            out_specs=[q_block, k_block, k_block],
-        ),
-        out_shape=[
-            jax.ShapeDtypeStruct((queries, pairs * PAIR), BF),
-            jax.ShapeDtypeStruct((keys, pairs * PAIR), BF),
-            jax.ShapeDtypeStruct((keys, pairs * PAIR), BF),
-        ],
-        compiler_params=attn_params(),
-        cost_estimate=pl.CostEstimate(
-            flops=16 * queries * keys * 256 * 10,
-            bytes_accessed=16 * queries * 1024,
-            transcendentals=16 * queries * keys,
-        ),
+        (pairs,),
+        [
+            (q_arr, pl.BlockSpec((queries, PAIR), lambda p, _: (0, q_at + p))),
+            (kv, pl.BlockSpec((keys, PAIR), lambda p, _: (0, k_at + p))),
+            (kv, pl.BlockSpec((keys, PAIR), lambda p, _: (0, v_at + p))),
+            (o, q_block),
+            (do, q_block),
+            (lse, pl.BlockSpec((1, 2, queries), lambda p, _: (p, 0, 0))),
+        ],
+        [
+            (shaped((queries, pairs * PAIR), BF), q_block),
+            (shaped((keys, pairs * PAIR), BF), k_block),
+            (shaped((keys, pairs * PAIR), BF), k_block),
+        ],
+        prefetch=(limit,),
+        deps=deps,
+        cost=costs(16 * queries * keys * 2560, 16 * queries * 1024, 16 * queries * keys),
         name="attn_bwd",
-    )(limit, q_arr, kv, kv, o, do, lse)
+    )
 
 
 def norm_parts(v):
@@ -212,7 +228,7 @@
     return lax.psum_scatter(part, "gx", scatter_dimension=0, tiled=True)
 
 
-def shards(
+def shards_any(
     hidden,
     memory,
     lengths,
@@ -366,11 +382,513 @@
     )
 
 
+CORE, XBIT, YBIT = 1, 2, 4
+
+
+def swap(a, bit):
+    return lax.ppermute(a, ALL, [(i, i ^ bit) for i in range(32)])
+
+
+def part_kernel(lo, src, out):
+    out[...] = src[lo : lo + 2]
+
+
+def part_of(piece, lo, deps):
+    _, rows, columns = piece.shape
+    block = 640 if columns % 640 == 0 else 1024
+    return run(
+        functools.partial(part_kernel, lo),
+        (columns // block,),
+        [(piece, pl.BlockSpec((4, rows, block), lambda j: (0, 0, j)))],
+        [(shaped((2, rows, columns), BF), pl.BlockSpec((2, rows, block), lambda j: (0, 0, j)))],
+        deps=deps,
+        cost=costs(0, 12 * rows * columns),
+        name="part_of",
+    )
+
+
+def gather_start(w):
+    here = lax.all_gather(w, "gx", axis=0)
+    return here, swap(here, XBIT), swap(here, YBIT)
+
+
+def gather_end(pieces, deps=()):
+    here, from_x, from_y = pieces
+    if deps:
+        low, high = part_of(from_y, 0, deps), part_of(from_x, 2, deps)
+    else:
+        low, high = from_y[:2], from_x[2:]
+    own = [here, from_x, from_y, swap(low, XBIT), swap(high, YBIT)]
+    return own + [swap(p, CORE) for p in own]
+
+
+def place_kernel(by_core, bits_ref, *refs):
+    out = refs[-1]
+    x, y, core = bits_ref[0], bits_ref[1], bits_ref[2]
+    for k in range(10):
+        at_core = core if k < 5 else 1 - core
+        at_x = x if k % 5 in (0, 2) else 1 - x
+        at_y = y if k % 5 in (0, 1) else 1 - y
+        z0, z1 = {3: (0, 2), 4: (2, 4)}.get(k % 5, (0, 4))
+        if by_core:
+            out[at_core * 4 + at_y * 2 + at_x, z0:z1] = refs[k][...]
+        else:
+            out[z0:z1, at_y * 4 + at_x * 2 + at_core] = refs[k][...]
+
+
+def place(pieces, start, width, bits, by_core=False, deps=()):
+    rows = pieces[0].shape[1]
+    block = min(width, 512)
+    lead = (8, 4) if by_core else (4, 8)
+    out = run(
+        functools.partial(place_kernel, by_core),
+        (width // block,),
+        [
+            (p, pl.BlockSpec((p.shape[0], rows, block), lambda j, _: (0, 0, start // block + j)))
+            for p in pieces
+        ],
+        [
+            (
+                shaped(lead + (rows, width), BF),
+                pl.BlockSpec(lead + (rows, block), lambda j, _: (0, 0, 0, j)),
+            )
+        ],
+        prefetch=(bits,),
+        deps=deps,
+        cost=costs(0, 4 * 32 * rows * width),
+        name="place",
+    )
+    return out.reshape(32 * rows, width)
+
+
+def wgrad_kernel(starts, *refs):
+    out = refs[-1]
+    j = pl.program_id(0)
+    for s in range(len(starts) - 1):
+        a, a2, g, g2 = refs[4 * s : 4 * s + 4]
+
+        @pl.when((j >= starts[s]) & (j < starts[s + 1]))
+        def _(a=a, a2=a2, g=g, g2=g2):
+            out[...] = (dot(a[...], g[...]) + dot(a2[...], g2[...])).astype(BF)
+
+
+def wgrad(segments, deps=(), block=512):
+    starts, ins = [0], []
+    for a, a2, g, g2 in segments:
+        per = g.shape[2] // block
+        count, start = g.shape[0] * per, starts[-1]
+
+        def at(j, start=start, count=count, per=per):
+            k = jnp.clip(j - start, 0, count - 1)
+            return (k // per, 0, k % per)
+
+        whole = pl.BlockSpec(a.shape, lambda j: (0, 0))
+        grads = pl.BlockSpec((None, g.shape[1], block), at)
+        ins += [(a, whole), (a2, whole), (g, grads), (g2, grads)]
+        starts.append(start + count)
+    rows = segments[0][0].shape[0]
+    columns = starts[-1] * block
+    return run(
+        functools.partial(wgrad_kernel, tuple(starts)),
+        (starts[-1],),
+        ins,
+        [(shaped((rows, columns), BF), pl.BlockSpec((rows, block), lambda j: (0, j)))],
+        deps=deps,
+        cost=costs(2 * rows * 1024 * columns, 4 * 512 * columns + 2 * rows * columns),
+        name="wgrad",
+    )
+
+
+def wgrad_down_kernel(bits_ref, *refs):
+    blocks, other, dy, dy2, out = refs[:4], refs[4:8], refs[8], refs[9], refs[10]
+    mine = jnp.concatenate([r[...].T for r in blocks], axis=0)
+    theirs = jnp.concatenate([r[...].T for r in other], axis=0)
+    out[...] = (dot(mine, dy[...]) + dot(theirs, dy2[...])).astype(BF)
+
+
+def wgrad_down(bits, g, g_other, dy, dy_other, cuts):
+    tokens, d = dy.shape
+
+    def spec(rel, whole):
+        def at(b, bits_ref):
+            x = bits_ref[0] ^ (rel & 1)
+            y = bits_ref[1] ^ (rel >> 1)
+            block = b * 4 + y * 2 + x
+            return (0, bits_ref[2] * 4 * cuts + block if whole else block)
+
+        return pl.BlockSpec((tokens, 128), at)
+
+    rows = pl.BlockSpec((tokens, d), lambda b, _: (0, 0))
+    return run(
+        wgrad_down_kernel,
+        (cuts,),
+        [(g, spec(r, True)) for r in range(4)]
+        + [(g_other, spec(r, False)) for r in range(4)]
+        + [(dy, rows), (dy_other, rows)],
+        [(shaped((512, cuts * d), BF), pl.BlockSpec((512, d), lambda b, _: (0, b)))],
+        prefetch=(bits,),
+        cost=costs(2 * 512 * 1024 * cuts * d, 16 * tokens * d),
+        name="wgrad_down",
+    )
+
+
+def up_kernel(h_ref, w_ref, g_ref, slope_ref):
+    u = dot(h_ref[...], w_ref[...])
+    cdf = 0.5 * (1.0 + lax.erf(u * (0.5**0.5)))
+    g_ref[...] = (u * cdf).astype(BF)
+    slope_ref[...] = (cdf + u * (jnp.exp(-0.5 * u * u) * 0.3989422804014327)).astype(BF)
+
+
+def feed_up(h, w, block=512):
+    tokens, d = h.shape
+    ff = w.shape[1]
+    out = (shaped((tokens, ff), BF), pl.BlockSpec((tokens, block), lambda j: (0, j)))
+    return run(
+        up_kernel,
+        (ff // block,),
+        [
+            (h, pl.BlockSpec((tokens, d), lambda j: (0, 0))),
+            (w, pl.BlockSpec((d, block), lambda j: (0, j))),
+        ],
+        [out, out],
+        cost=costs(2 * tokens * d * ff, 2 * d * ff + 4 * tokens * ff, 2 * tokens * ff),
+        name="feed_up",
+    )
+
+
+def down_kernel(g_ref, w_ref, x_ref, out_ref):
+    @pl.when(pl.program_id(0) == 0)
+    def _():
+        out_ref[...] = x_ref[...]
+
+    out_ref[...] += dot(g_ref[...], w_ref[...])
+
+
+def feed_down(g, w, x, cuts, deps=()):
+    tokens, d = x.shape
+    block = d // 2
+    whole = pl.BlockSpec((tokens, d), lambda j: (0, 0))
+    return run(
+        down_kernel,
+        (2 * cuts,),
+        [
+            (g, pl.BlockSpec((tokens, block), lambda j: (0, j))),
+            (w, pl.BlockSpec((block, d), lambda j: (j // cuts, j % cuts))),
+            (x, whole),
+        ],
+        [(shaped((tokens, d), F32), whole)],
+        deps=deps,
+        cost=costs(2 * tokens * d * d * cuts, 2 * d * d * cuts + 10 * tokens * d),
+        name="feed_down",
+    )
+
+
+def norm_back_store(dh, x_ref, gain_ref, res_ref, dx_ref, low_ref, sums_ref):
+    x = x_ref[...]
+    center = x - jnp.mean(x, -1, keepdims=True)
+    inverse = lax.rsqrt(jnp.mean(center * center, -1, keepdims=True) + 1e-05)
+    unit = center * inverse
+    sums_ref[0:1, :] = jnp.sum(dh * unit, axis=0, keepdims=True)
+    sums_ref[1:2, :] = jnp.sum(dh, axis=0, keepdims=True)
+    scaled = dh * gain_ref[...]
+    mean_a = jnp.mean(scaled, -1, keepdims=True)
+    mean_b = jnp.mean(scaled * unit, -1, keepdims=True)
+    dx = res_ref[...] + inverse * (scaled - mean_a - unit * mean_b)
+    dx_ref[...] = dx
+    if low_ref is not None:
+        low_ref[...] = dx.astype(BF)
+
+
+def accumulate(acc, part):
+    j = pl.program_id(0)
+
+    @pl.when(j == 0)
+    def _():
+        acc[...] = part
+
+    @pl.when(j > 0)
+    def _():
+        acc[...] += part
+
+
+def feed_back_kernel(
+    dy_ref, w2_ref, slope_ref, w1_ref, x_ref, gain_ref, res_ref, du_ref, dx_ref, low_ref, sums_ref, acc
+):
+    du = (dot_nt(dy_ref[...], w2_ref[...]) * slope_ref[...].astype(F32)).astype(BF)
+    du_ref[...] = du
+    accumulate(acc, dot_nt(du, w1_ref[...]))
+
+    @pl.when(pl.program_id(0) == pl.num_programs(0) - 1)
+    def _():
+        norm_back_store(acc[...], x_ref, gain_ref, res_ref, dx_ref, low_ref, sums_ref)
+
+
+def feed_back(dy, w2, slope, w1, x, gain, res, cuts, deps=()):
+    tokens, d = x.shape
+    block = d // 2
+    ff = w1.shape[1]
+    whole = pl.BlockSpec((tokens, d), lambda j: (0, 0))
+    part = pl.BlockSpec((tokens, block), lambda j: (0, j))
+    return run(
+        feed_back_kernel,
+        (2 * cuts,),
+        [
+            (dy, whole),
+            (w2, pl.BlockSpec((block, d), lambda j: (j // cuts, j % cuts))),
+            (slope, part),
+            (w1, pl.BlockSpec((d, block), lambda j: (0, j))),
+            (x, whole),
+            (gain, pl.BlockSpec((1, d), lambda j: (0, 0))),
+            (res, whole),
+        ],
+        [
+            (shaped((tokens, ff), BF), part),
+            (shaped((tokens, d), F32), whole),
+            (shaped((tokens, d), BF), whole),
+            (shaped((2, d), F32), pl.BlockSpec((2, d), lambda j: (0, 0))),
+        ],
+        scratch=[pltpu.VMEM((tokens, d), F32)],
+        deps=deps,
+        cost=costs(4 * tokens * d * ff, 4 * d * ff + 4 * tokens * ff + 16 * tokens * d),
+        name="feed_back",
+    )
+
+
+def norm_back_kernel(g_ref, w_ref, x_ref, gain_ref, res_ref, *refs):
+    dx_ref, sums_ref, acc = refs[0], refs[-2], refs[-1]
+    low_ref = refs[1] if len(refs) == 4 else None
+    accumulate(acc, dot_nt(g_ref[...], w_ref[...]))
+
+    @pl.when(pl.program_id(0) == pl.num_programs(0) - 1)
+    def _():
+        norm_back_store(acc[...], x_ref, gain_ref, res_ref, dx_ref, low_ref, sums_ref)
+
+
+def through_norm(g, w, x, gain, res, low=True, deps=()):
+    tokens, d = x.shape
+    block = 512
+    per = g.shape[2] // block
+    count = g.shape[0] * per
+    whole = pl.BlockSpec((tokens, d), lambda j: (0, 0))
+    outs = [(shaped((tokens, d), F32), whole)]
+    if low:
+        outs.append((shaped((tokens, d), BF), whole))
+    outs.append((shaped((2, d), F32), pl.BlockSpec((2, d), lambda j: (0, 0))))
+    return run(
+        norm_back_kernel,
+        (count,),
+        [
+            (g, pl.BlockSpec((None, tokens, block), lambda j: (j // per, 0, j % per))),
+            (w, pl.BlockSpec((d, block), lambda j: (0, j))),
+            (x, whole),
+            (gain, pl.BlockSpec((1, d), lambda j: (0, 0))),
+            (res, whole),
+        ],
+        outs,
+        scratch=[pltpu.VMEM((tokens, d), F32)],
+        deps=deps,
+        cost=costs(2 * tokens * d * block * count, 2 * d * block * count + 16 * tokens * d),
+        name="through_norm",
+    )
+
+
+def scatter_diag(grad, rows):
+    parts = grad.reshape(4, 4, rows, grad.shape[1])
+    from_x, from_y = swap(parts[3, :2], XBIT), swap(parts[3, 2:], YBIT)
+    to_x = jnp.concatenate([parts[1, :2], parts[1, 2:] + from_y], axis=0)
+    to_y = jnp.concatenate([parts[2, :2] + from_x, parts[2, 2:]], axis=0)
+    return parts[0], to_x, to_y
+
+
+def scatter_plane(stage):
+    here, to_x, to_y = stage
+    got_x, got_y = swap(to_x, XBIT), swap(to_y, YBIT)
+    total = here.astype(F32) + got_x.astype(F32) + got_y.astype(F32)
+    return total.astype(BF).reshape(-1, here.shape[2])
+
+
+def scatter_line(total):
+    return lax.psum_scatter(total, "gx", scatter_dimension=0, tiled=True)
+
+
+def shards_plane(
+    hidden,
+    memory,
+    lengths,
+    page_class,
+    cotangent,
+    w_self_qkv,
+    w_self_out,
+    w_cross_q,
+    w_cross_kv,
+    w_cross_out,
+    w_fc1,
+    w_fc2,
+    norm_gains,
+    norm_biases,
+):
+    tokens, d = hidden.shape
+    rows, ff = w_fc1.shape
+    cuts = w_fc2.shape[0] // rows
+    mem_rows = -(-memory.shape[0] // 16) * 16
+    slots_used = jnp.where(page_class == 0, MEM_BIG, MEM_BIG // 4).astype(jnp.int32)
+    along = lax.axis_index("gy")
+    x_at, y_at, core = (along // 2) % 2, along // 4, along % 2
+    bits = jnp.stack([x_at, y_at, core]).astype(jnp.int32)
+
+    norm_cols = jnp.concatenate([norm_gains, norm_biases], axis=0).T
+    norm_cols = jnp.pad(norm_cols, ((0, 0), (0, 128 - norm_cols.shape[1])))
+    up_local = (
+        w_fc1.reshape(rows, 4, 2, 2, 2, cuts, rows)
+        .transpose(0, 4, 5, 2, 3, 1, 6)
+        .reshape(rows, ff)
+    )
+    down_local = jnp.concatenate(
+        [w_fc2[c * rows : (c + 1) * rows] for c in range(cuts)], axis=1
+    )
+    first = gather_start(jnp.concatenate([w_self_qkv, norm_cols], axis=1))
+    second = gather_start(
+        jnp.concatenate([w_cross_kv, w_self_out, w_cross_q, w_cross_out], axis=1)
+    )
+    third = gather_start(up_local)
+    fourth = gather_start(down_local)
+
+    place_at = jnp.arange(d)
+    r = place_at % rows
+    z = (place_at // rows) % 4
+    rel = (place_at // (4 * rows)) % 4
+    source_core = core ^ (place_at // (16 * rows))
+    device = z * 8 + (y_at ^ (rel // 2)) * 4 + (x_at ^ (rel % 2)) * 2 + source_core
+    select = ((device * rows + r)[:, None] == place_at[None, :]).astype(BF)
+    half = d // 2
+
+    def turned(a):
+        t = dot_nt(select, a).astype(BF)
+        return t[:half], swap(t[half:], CORE)
+
+    first = gather_end(first)
+    wqkv = place(first, 0, 3 * d, bits)
+    norms = place(first, 3 * d, 128, bits)[:, :6].T.astype(F32)
+    gains, biases = norms[:3], norms[3:]
+    unit1, _ = norm_parts(hidden)
+    h1 = (unit1 * gains[0] + biases[0]).astype(BF)
+    qkv = dot(h1, wqkv).astype(BF)
+    blocks = d // PAIR
+    o, lse = attn_fwd((qkv, 0), qkv, blocks, 2 * blocks, lengths, True)
+    second = gather_end(second, (qkv,))
+    wckv = place(second, 0, 2 * d, bits, deps=(o,))
+    wso, wcq, wco = (place(second, k * d, d, bits, deps=(o,)) for k in (2, 3, 4))
+    x1 = hidden + dot(o, wso)
+    unit2, _ = norm_parts(x1)
+    h2 = (unit2 * gains[1] + biases[1]).astype(BF)
+    qc = dot(h2, wcq).astype(BF)
+    third = gather_end(third, (qc,))
+    memory_pad = jnp.pad(memory, ((0, mem_rows - memory.shape[0]), (0, 0)))
+    kvc = dot(memory_pad, wckv).astype(BF)
+    o2, lse2 = attn_fwd((qc, 0), kvc, 0, blocks, slots_used, False)
+    x2 = x1 + dot(o2, wco)
+    unit3, _ = norm_parts(x2)
+    h3 = (unit3 * gains[2] + biases[2]).astype(BF)
+    fourth = gather_end(fourth, (h3,))
+    wup = place(third, 0, ff, bits, deps=(o2,))
+    g, slope = feed_up(h3, wup)
+    h1_t, o_t, h2_t, o2_t, h3_t = turned(h1), turned(o), turned(h2), turned(o2), turned(h3)
+    mem_t = turned(memory_pad)
+
+    valid = (jnp.arange(tokens) < lengths[0])[:, None].astype(F32)
+    dout = cotangent * valid
+    dy3 = dout.astype(BF)
+    g_other = swap(lax.dynamic_slice_in_dim(g, (1 - core) * (ff // 2), ff // 2, 1), CORE)
+    dy3_other = swap(dy3, CORE)
+    grad_down = wgrad_down(bits, g, g_other, dy3, dy3_other, cuts)
+    wdown = place(fourth, 0, cuts * d, bits, True, deps=(grad_down,))
+    stage1 = scatter_diag(grad_down, rows)
+    du, dx2, dy2, sums3 = feed_back(dy3, wdown, slope, wup, x2, gains[2:3], dout, cuts)
+    do2 = dot_nt(dy2, wco).astype(BF)
+    dqc, dkc, dvc = attn_bwd(
+        (qc, 0), kvc, 0, blocks, o2, do2, lse2, slots_used, False, deps=stage1[1:]
+    )
+    dkvc = jnp.stack([dkc, dvc])
+    grad_up = wgrad([h3_t + (du[None], swap(du, CORE)[None])], deps=(dqc,))
+    stage2 = scatter_diag(grad_up, rows)
+    dx1, dy1, sums2 = through_norm(
+        dqc[None], wcq, x1, gains[1:2], dx2, deps=(grad_up,)
+    )
+    total1 = scatter_plane(stage1)
+    own_down = scatter_line(total1)
+    grad_mid = wgrad(
+        [
+            o2_t + (dy2[None], swap(dy2, CORE)[None]),
+            h2_t + (dqc[None], swap(dqc, CORE)[None]),
+            mem_t + (dkvc, swap(dkvc, CORE)),
+        ],
+        deps=(total1, dy1),
+    )
+    stage3 = scatter_diag(grad_mid, rows)
+    do = dot_nt(dy1, wso).astype(BF)
+    dqkv = jnp.stack(
+        attn_bwd(
+            (qkv, 0), qkv, blocks, 2 * blocks, o, do, lse, lengths, True,
+            deps=stage2[1:] + (grad_mid,),
+        )
+    )
+    total2 = scatter_plane(stage2)
+    own_up = scatter_line(total2)
+    grad_hidden, sums1 = through_norm(dqkv, wqkv, hidden, gains[0:1], dx1, low=False)
+    sums = jnp.concatenate([sums1, sums2, sums3], axis=0)
+    sums = jnp.pad(sums, ((0, 122), (0, 0))).astype(BF)
+    sums_t, sums_other = turned(sums)
+    grad_last = jnp.concatenate(
+        [
+            wgrad(
+                [
+                    o_t + (dy1[None], swap(dy1, CORE)[None]),
+                    h1_t + (dqkv, swap(dqkv, CORE)),
+                ],
+                deps=stage3[1:] + (total2,),
+            ),
+            (sums_t.astype(F32) + sums_other.astype(F32)).astype(BF),
+        ],
+        axis=1,
+    )
+    own_mid = scatter_line(scatter_plane(stage3))
+    stage4 = scatter_diag(grad_last, rows)
+    result = feed_down(g, wdown, x2, cuts, deps=(grad_last,))
+    own_last = scatter_line(scatter_plane(stage4))
+    grad_memory = (dot_nt(dkc, wckv[:, :d]) + dot_nt(dvc, wckv[:, d:]))[: memory.shape[0]]
+
+    own_up = (
+        own_up.reshape(rows, 2, cuts, 2, 2, 4, rows)
+        .transpose(0, 5, 3, 4, 1, 2, 6)
+        .reshape(rows, ff)
+    )
+    own_down = jnp.concatenate(
+        [own_down[:, c * d : (c + 1) * d] for c in range(cuts)], axis=0
+    )
+    own_sums = own_last[:, 4 * d : 4 * d + 6].T.astype(F32)
+    return (
+        result,
+        grad_hidden,
+        grad_memory,
+        own_last[:, d : 4 * d].astype(F32),
+        own_last[:, :d].astype(F32),
+        own_mid[:, d : 2 * d].astype(F32),
+        own_mid[:, 2 * d :].astype(F32),
+        own_mid[:, :d].astype(F32),
+        own_up.astype(F32),
+        own_down.astype(F32),
+        own_sums[0::2],
+        own_sums[1::2],
+    )
+
+
 def solution(mesh):
     row = P(ALL, None)
     col = P(None, ALL)
+    nx, ny = mesh.shape["gx"], mesh.shape["gy"]
+    body = shards_plane if (nx, ny) == (4, 8) else functools.partial(shards_any, nx=nx, ny=ny)
     return jax.shard_map(
-        functools.partial(shards, nx=mesh.shape["gx"], ny=mesh.shape["gy"]),
+        body,
         mesh=mesh,
         in_specs=(row, row, P(ALL), P(ALL), row) + (row,) * 7 + (col, col),
         out_specs=(row,) * 10 + (col, col),

time: 789 us -> 582 us (0.74)
  waiting for transfers between devices: 464 us -> 121 us
  Pallas kernels: 63.1 us -> 217 us
  matrix products: 143 us -> 43.4 us
  starting transfers between devices: 0.74 us -> 42.1 us
  blocking collectives: 0 us -> 29 us
    all_gather x4 -> x3, waiting for transfers between devices: 243 us -> 0.01 us  [gather_start(): here = lax.all_gather(w, 'gx', axis=0)]
    reduce_scatter x6 -> x4, waiting for transfers between devices: 200 us -> 6.21 us  [scatter_line(): return lax.psum_scatter(total, 'gx', scatter_dimension=0, tiled=True)]
    pallas_call x4 -> x27, Pallas kernels: 63.1 us -> 217 us  [run(): pl.pallas_call(body, grid_spec=pltpu.PrefetchScalarGridSpec(num_scalar_pr...]
    ppermute x0 -> x67, waiting for transfers between devices: none -> 115 us  [swap(): return lax.ppermute(a, ALL, [(i, i ^ bit) for i in range(32)])]
    dot_general x16 -> x5, matrix products: 88.9 us -> 21 us  [dot(): return jnp.dot(a, b, preferred_element_type=F32)]
    ppermute x0 -> x67, starting transfers between devices: none -> 41.8 us  [swap(): return lax.ppermute(a, ALL, [(i, i ^ bit) for i in range(32)])]
    all_gather x0 -> x1, blocking collectives: none -> 29 us  [gather_start(): here = lax.all_gather(w, 'gx', axis=0)]
    dot_general x11, matrix products: 46.9 us -> 22.4 us  [dot_nt(): lax.dot_general(a, b, (((1,), (1,)), ((), ())), preferred_element_type=F32)]
  transfers between devices with their start and end apart: 12 -> 74, of which waited for: 10 -> 14; matrix products, arithmetic and copies ran while one was open for 25% -> 21% of each run, Pallas kernels for 8% -> 38%
where the time goes in v2:
time: 582 us; the launch traced here: 573 us
  Pallas kernels  217 us (37%)
  waiting for transfers between devices  121 us (21%)
  local copies, waits for them, and re-layouts  60.2 us (10%)
  other arithmetic  43.4 us (7%)
  matrix products  43.4 us (7%)
  starting transfers between devices  42.1 us (7%)
  blocking collectives  29 us (5%)
  between operations  17 us (3%)
    pallas_call x27, Pallas kernels, run(): pl.pallas_call(body, grid_spec=pltpu.PrefetchScalarGridSpec(num_scalar_pr...  217 us
    ppermute x67, waiting for transfers between devices, swap(): return lax.ppermute(a, ALL, [(i, i ^ bit) for i in range(32)])  115 us
    ppermute x67, starting transfers between devices, swap(): return lax.ppermute(a, ALL, [(i, i ^ bit) for i in range(32)])  41.8 us
    all_gather x1, blocking collectives, gather_start(): here = lax.all_gather(w, 'gx', axis=0)  29 us
    dot_general x11, matrix products, dot_nt(): lax.dot_general(a, b, (((1,), (1,)), ((), ())), preferred_element_type=F32)  22.4 us
    dot_general x5, matrix products, dot(): return jnp.dot(a, b, preferred_element_type=F32)  21 us
    unnamed x142, local copies, waits for them, and re-layouts  20.6 us
  transfers between devices with their start and end apart: 74, of which 14 were waited for; matrix products, arithmetic and copies ran while one was open for 21% of the time, Pallas kernels for 38%

profile of v2, /device:TPU:0, one launch (start us, length us, event | category | flops | bytes accessed | tf_op | source)
XLA Modules:
  0.0 572.8 jit_solution(6061606648185273226)
XLA Ops:
  9.6 1.8 all_gather_reshape.3
  12.5 29.0 %all-gather = bf16[128,3200]{1,0:T(8,128)(2,1)S(1)} all-gather(bf16[32,3200]{1,0:T(8,128)(2,1)S(1)} %fusion.57), channel_id=2, replica_groups=mesh['gx'=4,'gy'=8] {'gx'}, dimensions={0}, use_global_device_ids=true | all-gather | bytes 1024000 | tf_op jit(solution)/shard_map/all_gather | solution.py:411
  45.3 3.3 fusion.26
  49.8 9.5 %collective-permute-done.1.refs_3_ = bf16[4,32,3200]{2,1,0:T(8,128)(2,1)} collective-permute-done((bf16[4,32,3200]{2,1,0:T(8,128)(2,1)S(1)}, bf16[4,32,3200]{2,1,0:T(8,128)(2,1)}, u32[]{:S(2)}, u32[]{:S(2)}) %collective-permute-start.1) | collective-permute-done | bytes 819232 | tf_op jit(solution)/shard_map/ppermute | solution.py:389
  61.8 1.8 slice.296
  66.8 2.2 copy.47
  69.3 2.6 collective-permute-done.3.refs_5_
  77.2 7.4 %place.9 = bf16[4,8,32,3072]{3,2,1,0:T(8,128)(2,1)} custom-call(s32[3]{0:T(128)S(1)} %pad_add_fusion.refs_0_, bf16[4,32,3200]{2,1,0:T(8,128)(2,1)S(1)} %bitcast.146, bf16[4,32,3200]{2,1,0:T(8,128)(2,1)} %collective-permute-done.refs_2_, bf16[4,32,3200]{2,1,0:T(8,128)(2,1)} %collective-permute-done.1.refs_3_, ...), custom_call_target="tpu_custom_call" | custom-call | bytes 12582912 | tf_op jit(solution)/shard_map/place/pallas_call | solution.py:36
  86.8 7.0 %convolution_convert_fusion.refs_1_.refs_2_.refs_3_ = bf16[512,3072]{1,0:T(8,128)(2,1)S(1)} fusion(bf16[1024,3072]{1,0:T(8,128)(2,1)} %bitcast.172, f32[512,1024]{1,0:T(8,128)} %refs_2_.1, f32[1024]{0:T(1024)S(1)} %bitcast.207, f32[1024]{0:T(1024)S(1)} %bitcast.161, f32[512]{0:T(512)S(1)} %add_rsqrt_fusion.2, f32[512]{0:T(512)S(1)} %broadcast_multiply_fusion.3), kind=kOutput, calls=%fused_computation.2 | convolution fusion | flops 3225419776 | bytes 11546624 | tf_op jit(solution)/shard_map/dot_general | solution.py:19
  93.8 33.5 %collective-permute-done.10.refs_0_.refs_3_ = bf16[4,32,5120]{2,1,0:T(8,128)(2,1)S(1)} collective-permute-done((bf16[4,32,5120]{2,1,0:T(8,128)(2,1)}, bf16[4,32,5120]{2,1,0:T(8,128)(2,1)S(1)}, u32[]{:S(2)}, u32[]{:S(2)}) %collective-permute-start.10) | collective-permute-done | bytes 1310752 | tf_op jit(solution)/shard_map/ppermute | solution.py:389
  127.3 2.8 part_of.6
  131.0 2.7 part_of.7
  135.5 2.0 fusion.93
  137.5 2.1 copy.48.refs_9_
  139.7 1.9 copy-done.11
  141.6 13.5 %attn_fwd.2 = (bf16[512,1024]{1,0:T(8,128)(2,1)S(1)}, f32[8,2,512]{2,1,0:T(2,128)S(1)}) custom-call(s32[1]{0:T(128)} %copy.59.refs_0_, bf16[512,3072]{1,0:T(8,128)(2,1)S(1)} %copy-done.11, bf16[512,3072]{1,0:T(8,128)(2,1)S(1)} %copy-done.11, bf16[512,3072]{1,0:T(8,128)(2,1)S(1)} %copy-done.11), custom_call_target="tpu_custom_call" | custom-call | flops 4294967296 | bytes 4194304 | tf_op jit(solution)/shard_map/attn_fwd/pallas_call | solution.py:36
  155.7 2.3 fusion.27
  158.0 2.5 fusion.29
  161.1 3.2 place.10
  164.3 3.0 fusion.103
  167.7 5.4 place.12
  173.0 5.1 convolution_convert_fusion.1.refs_2_.refs_3_
  178.1 3.8 place.11
  182.0 2.9 convolution_convert_fusion.4.refs_1_
  185.0 2.4 part_of.8
  189.0 2.1 part_of.9
  191.6 17.6 %attn_fwd.3 = (bf16[512,1024]{1,0:T(8,128)(2,1)S(1)}, f32[8,2,512]{2,1,0:T(2,128)S(1)}) custom-call(s32[1]{0:T(128)S(6)} %select_n.97.refs_0_, bf16[512,1024]{1,0:T(8,128)(2,1)S(1)} %convolution_convert_fusion.4.refs_1_, bf16[592,2048]{1,0:T(8,128)(2,1)S(1)} %convolution_convert_fusion.1.refs_2_.refs_3_, ...), custom_call_target="tpu_custom_call" | custom-call | flops 4966055936 | bytes 4194304 | tf_op jit(solution)/shard_map/attn_fwd/pallas_call | solution.py:36
  209.2 3.6 place.13
  212.9 3.0 fusion.104
  220.8 9.1 %place.14 = bf16[4,8,32,4096]{3,2,1,0:T(8,128)(2,1)} custom-call(s32[3]{0:T(128)S(1)} %pad_add_fusion.refs_0_, bf16[4,32,4096]{2,1,0:T(8,128)(2,1)S(1)} %copy-done.24, bf16[4,32,4096]{2,1,0:T(8,128)(2,1)} %collective-permute-done.18.refs_0_.refs_2_, bf16[4,32,4096]{2,1,0:T(8,128)(2,1)} %collective-permute-done.19.refs_0_.refs_3_, ...), custom_call_target="tpu_custom_call" | custom-call | bytes 16777216 | tf_op jit(solution)/shard_map/place/pallas_call | solution.py:36
  229.9 11.9 %feed_up.1 = (bf16[512,4096]{1,0:T(8,128)(2,1)S(1)}, bf16[512,4096]{1,0:T(8,128)(2,1)}) custom-call(bf16[512,1024]{1,0:T(8,128)(2,1)S(1)} %add_convert_fusion.refs_0_.refs_1_, bf16[1024,4096]{1,0:T(8,128)(2,1)} %bitcast.182), custom_call_target="tpu_custom_call" | custom-call | flops 4294967296 | bytes 16777216 | tf_op jit(solution)/shard_map/feed_up/pallas_call | solution.py:36
  256.8 4.3 collective-permute-done.29.refs_4_
  263.1 9.2 %wgrad_down.1.refs_11_ = bf16[512,4096]{1,0:T(8,128)(2,1)} custom-call(s32[3]{0:T(128)S(1)} %pad_add_fusion.refs_0_, bf16[512,4096]{1,0:T(8,128)(2,1)} %copy-done, bf16[512,4096]{1,0:T(8,128)(2,1)} %copy-done, bf16[512,4096]{1,0:T(8,128)(2,1)} %copy-done, bf16[512,4096]{1,0:T(8,128)(2,1)} %copy-done, ...), custom_call_target="tpu_custom_call" | custom-call | flops 4294967296 | bytes 8388608 | tf_op jit(solution)/shard_map/wgrad_down/pallas_call | solution.py:36
  272.3 2.8 slice_bitcast_fusion.19
  277.0 8.2 %place.15 = bf16[8,4,32,4096]{3,2,1,0:T(8,128)(2,1)} custom-call(s32[3]{0:T(128)S(1)} %pad_add_fusion.refs_0_, bf16[4,32,4096]{2,1,0:T(8,128)(2,1)S(1)} %bitcast.153, bf16[4,32,4096]{2,1,0:T(8,128)(2,1)S(1)} %collective-permute-done.27.refs_0_.refs_2_, bf16[4,32,4096]{2,1,0:T(8,128)(2,1)S(1)} %collective-permute-done.28.refs_0_.refs_3_, ...), custom_call_target="tpu_custom_call" | custom-call | bytes 16777216 | tf_op jit(solution)/shard_map/place/pallas_call | solution.py:36
  285.2 19.4 %feed_back.1 = (bf16[512,4096]{1,0:T(8,128)(2,1)}, f32[512,1024]{1,0:T(8,128)S(1)}, bf16[512,1024]{1,0:T(8,128)(2,1)S(1)}, f32[2,1024]{1,0:T(2,128)S(1)}) custom-call(bf16[512,1024]{1,0:T(8,128)(2,1)} %get-tuple-element.90.refs_9_.refs_0_, bf16[1024,4096]{1,0:T(8,128)(2,1)} %bitcast.168, bf16[512,4096]{1,0:T(8,128)(2,1)} %get-tuple-element.36.refs_2_, ...), custom_call_target="tpu_custom_call" | custom-call | flops 8589934592 | bytes 33554432 | tf_op jit(solution)/shard_map/feed_back/pallas_call | solution.py:36
  304.8 2.2 copy-done.47
  313.5 18.3 %attn_bwd.2 = (bf16[512,1024]{1,0:T(8,128)(2,1)S(1)}, bf16[592,1024]{1,0:T(8,128)(2,1)}, bf16[592,1024]{1,0:T(8,128)(2,1)}) custom-call(s32[1]{0:T(128)S(6)} %select_n.97.refs_0_, bf16[512,1024]{1,0:T(8,128)(2,1)S(1)} %copy-done.15, bf16[592,2048]{1,0:T(8,128)(2,1)} %copy-done.34, bf16[592,2048]{1,0:T(8,128)(2,1)} %copy-done.34, ...), custom_call_target="tpu_custom_call" | custom-call | flops 12415139840 | bytes 8388608 | tf_op jit(solution)/shard_map/attn_bwd/pallas_call | solution.py:36
  331.8 3.7 pad_maximum_fusion.2.refs_10_
  339.5 10.5 %wgrad.3.refs_5_ = bf16[512,4096]{1,0:T(8,128)(2,1)} custom-call(bf16[512,512]{1,0:T(8,128)(2,1)S(1)} %copy-done.33, bf16[512,512]{1,0:T(8,128)(2,1)} %collective-permute-done.41.refs_1_, bf16[1,512,4096]{2,1,0:T(8,128)(2,1)} %bitcast.209, bf16[1,512,4096]{2,1,0:T(8,128)(2,1)} %bitcast.33.refs_3_, bf16[512,1024]{1,0:T(8,128)(2,1)S(1)} %get-tuple-element.39.refs_4_), custom_call_target="tpu_custom_call" | custom-call | flops 4294967296 | bytes 12582912 | tf_op jit(solution)/shard_map/wgrad/pallas_call | solution.py:36
  350.0 2.7 slice_bitcast_fusion.13
  352.7 6.1 %through_norm.2 = (f32[512,1024]{1,0:T(8,128)S(1)}, bf16[512,1024]{1,0:T(8,128)(2,1)S(1)}, f32[2,1024]{1,0:T(2,128)S(1)}) custom-call(bf16[1,512,1024]{2,1,0:T(8,128)(2,1)S(1)} %bitcast.148, bf16[1024,1024]{1,0:T(8,128)(2,1)} %bitcast.186, f32[512,1024]{1,0:T(8,128)} %copy-done.39, f32[1,1024]{1,0:T(1,128)S(1)} %get-tuple-element.141.refs_3_, ...), custom_call_target="tpu_custom_call" | custom-call | flops 1073741824 | bytes 10485760 | tf_op jit(solution)/shard_map/through_norm/pallas_call | solution.py:36
  363.2 11.6 %wgrad.4.refs_9_ = bf16[512,4096]{1,0:T(8,128)(2,1)} custom-call(bf16[512,512]{1,0:T(8,128)(2,1)S(1)} %get-tuple-element.125.refs_0_, bf16[512,512]{1,0:T(8,128)(2,1)} %collective-permute-done.47.refs_1_, bf16[1,512,1024]{2,1,0:T(8,128)(2,1)S(1)} %bitcast.154, bf16[1,512,1024]{2,1,0:T(8,128)(2,1)S(1)} %bitcast.155, ...), custom_call_target="tpu_custom_call" | custom-call | flops 4294967296 | bytes 12582912 | tf_op jit(solution)/shard_map/wgrad/pallas_call | solution.py:36
  374.8 2.9 slice_bitcast_fusion.7
  384.5 13.9 %attn_bwd.3 = (bf16[512,1024]{1,0:T(8,128)(2,1)S(1)}, bf16[512,1024]{1,0:T(8,128)(2,1)S(1)}, bf16[512,1024]{1,0:T(8,128)(2,1)S(1)}) custom-call(s32[1]{0:T(128)} %copy.59.refs_0_, bf16[512,3072]{1,0:T(8,128)(2,1)} %copy-done.10, bf16[512,3072]{1,0:T(8,128)(2,1)} %copy-done.10, bf16[512,3072]{1,0:T(8,128)(2,1)} %copy-done.10, ...), custom_call_target="tpu_custom_call" | custom-call | flops 10737418240 | bytes 8388608 | tf_op jit(solution)/shard_map/attn_bwd/pallas_call | solution.py:36
  398.4 2.1 pad_maximum_fusion.1.refs_6_.refs_0_
  400.6 11.1 %through_norm.3 = (f32[512,1024]{1,0:T(8,128)}, f32[2,1024]{1,0:T(2,128)S(1)}) custom-call(bf16[3,512,1024]{2,1,0:T(8,128)(2,1)} %pad_maximum_fusion.1.refs_6_.refs_0_, bf16[1024,3072]{1,0:T(8,128)(2,1)} %bitcast.173, f32[512,1024]{1,0:T(8,128)S(1)} %copy-done.5, f32[1,1024]{1,0:T(1,128)S(1)} %get-tuple-element.143.refs_3_, ...), custom_call_target="tpu_custom_call" | custom-call | flops 3221225472 | bytes 14680064 | tf_op jit(solution)/shard_map/through_norm/pallas_call | solution.py:36
  418.4 20.0 %collective-permute-done.58 = bf16[4,32,4096]{2,1,0:T(8,128)(2,1)S(1)} collective-permute-done((bf16[4,32,4096]{2,1,0:T(8,128)(2,1)S(1)}, bf16[4,32,4096]{2,1,0:T(8,128)(2,1)S(1)}, u32[]{:S(2)}, u32[]{:S(2)}) %collective-permute-start.58) | collective-permute-done | bytes 1048608 | tf_op jit(solution)/shard_map/ppermute | solution.py:389
  438.4 2.7 fusion.16
  447.0 10.0 %wgrad.5 = bf16[512,4096]{1,0:T(8,128)(2,1)} custom-call(bf16[512,512]{1,0:T(8,128)(2,1)S(1)} %copy-done.19, bf16[512,512]{1,0:T(8,128)(2,1)S(1)} %copy-done.30, bf16[1,512,1024]{2,1,0:T(8,128)(2,1)S(1)} %bitcast.147, bf16[1,512,1024]{2,1,0:T(8,128)(2,1)S(1)} %bitcast.156, bf16[512,512]{1,0:T(8,128)(2,1)S(1)} %copy-done.20, bf16[512,512]{1,0:T(8,128)(2,1)S(1)} %copy-done.32, ...), custom_call_target="tpu_custom_call" | custom-call | flops 4294967296 | bytes 12582912 | tf_op jit(solution)/shard_map/wgrad/pallas_call | solution.py:36
  457.0 2.5 pad_maximum_fusion.refs_3_
  466.7 10.0 %collective-permute-done.61 = bf16[2,32,4224]{2,1,0:T(8,128)(2,1)} collective-permute-done((bf16[2,32,4224]{2,1,0:T(8,128)(2,1)}, bf16[2,32,4224]{2,1,0:T(8,128)(2,1)}, u32[]{:S(2)}, u32[]{:S(2)}) %collective-permute-start.61) | collective-permute-done | bytes 540704 | tf_op jit(solution)/shard_map/ppermute | solution.py:389
  483.5 15.6 %collective-permute-done.66 = bf16[4,32,4096]{2,1,0:T(8,128)(2,1)} collective-permute-done((bf16[4,32,4096]{2,1,0:T(8,128)(2,1)S(1)}, bf16[4,32,4096]{2,1,0:T(8,128)(2,1)}, u32[]{:S(2)}, u32[]{:S(2)}) %collective-permute-start.66) | collective-permute-done | bytes 1048608 | tf_op jit(solution)/shard_map/ppermute | solution.py:389
  500.2 3.0 fusion.14
  503.3 3.6 fusion.9
  506.9 13.9 %collective-permute-done.64 = bf16[4,32,4224]{2,1,0:T(8,128)(2,1)} collective-permute-done((bf16[4,32,4224]{2,1,0:T(8,128)(2,1)}, bf16[4,32,4224]{2,1,0:T(8,128)(2,1)}, u32[]{:S(2)}, u32[]{:S(2)}) %collective-permute-start.64) | collective-permute-done | bytes 1081376 | tf_op jit(solution)/shard_map/ppermute | solution.py:389
  521.6 3.1 fusion.8
  524.7 3.4 fusion.11
  528.1 1.9 slice_add_fusion
  531.8 2.1 reshape.256
  533.9 2.1 copy.50
  536.0 4.6 reshape.255
  542.2 11.1 %feed_down.1 = f32[512,1024]{1,0:T(8,128)} custom-call(bf16[512,4096]{1,0:T(8,128)(2,1)} %copy-done, bf16[1024,4096]{1,0:T(8,128)(2,1)} %bitcast.169, f32[512,1024]{1,0:T(8,128)S(1)} %copy-done.7, bf16[512,4224]{1,0:T(8,128)(2,1)} %copy-done.37), custom_call_target="tpu_custom_call" | custom-call | flops 4294967296 | bytes 13631488 | tf_op jit(solution)/shard_map/feed_down/pallas_call | solution.py:36
  554.0 6.2 %reduce-scatter.5.cloned.1.call-done = bf16[32,4224]{1,0:T(8,128)(2,1)} async-done(((bf16[128,4224]{1,0:T(8,128)(2,1)}), bf16[32,4224]{1,0:T(8,128)(2,1)}) %reduce-scatter.5.cloned.1.call-update) | async-done | bytes 270352 | tf_op jit(solution)/shard_map/reduce_scatter | solution.py:711
  (358 shorter events, 110.3 us)
Async XLA Ops:
  7.2 65.6 %all-gather.7.cloned.1.call-start = ((), (), s32[]{:S(2)}) async-start(), calls=%async_computation.4 | async-start | bytes 1310720 | tf_op jit(solution)/shard_map/all_gather | solution.py:411
  11.4 73.2 %all-gather.9.cloned.1.call-start = ((), (), s32[]{:S(2)}) async-start(), calls=%async_computation.9 | async-start | bytes 1638400 | tf_op jit(solution)/shard_map/all_gather | solution.py:411
  12.3 205.1 %all-gather.11.cloned.1.call-start = ((), (), s32[]{:S(2)}) async-start(), calls=%async_computation.10 | async-start | bytes 1310720 | tf_op jit(solution)/shard_map/all_gather | solution.py:411
  41.5 20.3 %collective-permute-start = (bf16[4,32,3200]{2,1,0:T(8,128)(2,1)S(1)}, bf16[4,32,3200]{2,1,0:T(8,128)(2,1)}, u32[]{:S(2)}, u32[]{:S(2)}) collective-permute-start(bf16[4,32,3200]{2,1,0:T(8,128)(2,1)S(1)} %bitcast.142), channel_id=1, source_target_pairs={{0,2},{1,3},{2,0},{3,1},{4,6},{5,7},{6,4},{7,5},{8,10},{9,11},{10,... | collective-permute-start | bytes 2457608 | tf_op jit(solution)/shard_map/ppermute | solution.py:389
  43.0 16.3 %collective-permute-start.1 = (bf16[4,32,3200]{2,1,0:T(8,128)(2,1)S(1)}, bf16[4,32,3200]{2,1,0:T(8,128)(2,1)}, u32[]{:S(2)}, u32[]{:S(2)}) collective-permute-start(bf16[4,32,3200]{2,1,0:T(8,128)(2,1)S(1)} %bitcast.143), channel_id=1, source_target_pairs={{0,4},{1,5},{2,6},{3,7},{4,0},{5,1},{6,2},{7,3},{8,12},{9,13},{10,... | collective-permute-start | bytes 2457608 | tf_op jit(solution)/shard_map/ppermute | solution.py:389
  44.4 27.8 %collective-permute-start.4 = (bf16[4,32,3200]{2,1,0:T(8,128)(2,1)S(1)}, bf16[4,32,3200]{2,1,0:T(8,128)(2,1)}, u32[]{:S(2)}, u32[]{:S(2)}) collective-permute-start(bf16[4,32,3200]{2,1,0:T(8,128)(2,1)S(1)} %bitcast.144), channel_id=1, source_target_pairs={{0,1},{1,0},{2,3},{3,2},{4,5},{5,4},{6,7},{7,6},{8,9},{9,8},{10,11... | collective-permute-start | bytes 2457608 | tf_op jit(solution)/shard_map/ppermute | solution.py:389
  45.2 484.8 %reduce-scatter.11.cloned.1.call-start = ((), (), s32[]{:S(2)}) async-start(), calls=%async_computation.8 | async-start | bytes 1310720 | tf_op jit(solution)/shard_map/reduce_scatter | solution.py:711
  64.9 9.1 %collective-permute-start.6 = (bf16[4,32,3200]{2,1,0:T(8,128)(2,1)}, bf16[4,32,3200]{2,1,0:T(8,128)(2,1)}, u32[]{:S(2)}, u32[]{:S(2)}) collective-permute-start(bf16[4,32,3200]{2,1,0:T(8,128)(2,1)} %collective-permute-done.1.refs_3_), channel_id=1, source_target_pairs={{0,1},{1,0},{2,3},{3,2},{4,5},{5,4},{6,7},{7,6},{8,9},{9,8},{10,11... | collective-permute-start | bytes 2457608 | tf_op jit(solution)/shard_map/ppermute | solution.py:389
  72.2 61.4 %collective-permute-start.51 = (bf16[512,592]{0,1:T(8,128)(2,1)}, bf16[512,592]{0,1:T(8,128)(2,1)}, u32[]{:S(2)}, u32[]{:S(2)}) collective-permute-start(bf16[512,592]{0,1:T(8,128)(2,1)} %copy.47), channel_id=1, source_target_pairs={{0,1},{1,0},{2,3},{3,2},{4,5},{5,4},{6,7},{7,6},{8,9},{9,8},{10,11... | collective-permute-start | bytes 1818632 | tf_op jit(solution)/shard_map/ppermute | solution.py:389
  72.8 62.2 %collective-permute-start.18 = (bf16[4,32,4096]{2,1,0:T(8,128)(2,1)}, bf16[4,32,4096]{2,1,0:T(8,128)(2,1)}, u32[]{:S(2)}, u32[]{:S(2)}) collective-permute-start(bf16[4,32,4096]{2,1,0:T(8,128)(2,1)} %all-gather.7.cloned.1.call-done.refs_1_), channel_id=1, source_target_pairs={{0,2},{1,3},{2,0},{3,1},{4,6},{5,7},{6,4},{7,5},{8,10},{9,11},{10,... | collective-permute-start | bytes 3145736 | tf_op jit(solution)/shard_map/ppermute | solution.py:389
  74.1 60.9 %collective-permute-start.19 = (bf16[4,32,4096]{2,1,0:T(8,128)(2,1)}, bf16[4,32,4096]{2,1,0:T(8,128)(2,1)}, u32[]{:S(2)}, u32[]{:S(2)}) collective-permute-start(bf16[4,32,4096]{2,1,0:T(8,128)(2,1)} %all-gather.7.cloned.1.call-done.refs_1_), channel_id=1, source_target_pairs={{0,4},{1,5},{2,6},{3,7},{4,0},{5,1},{6,2},{7,3},{8,12},{9,13},{10,... | collective-permute-start | bytes 3145736 | tf_op jit(solution)/shard_map/ppermute | solution.py:389
  84.7 45.4 %collective-permute-start.9 = (bf16[4,32,5120]{2,1,0:T(8,128)(2,1)}, bf16[4,32,5120]{2,1,0:T(8,128)(2,1)S(1)}, u32[]{:S(2)}, u32[]{:S(2)}) collective-permute-start(bf16[4,32,5120]{2,1,0:T(8,128)(2,1)} %bitcast.10.refs_1_), channel_id=1, source_target_pairs={{0,2},{1,3},{2,0},{3,1},{4,6},{5,7},{6,4},{7,5},{8,10},{9,11},{10,... | collective-permute-start | bytes 3932168 | tf_op jit(solution)/shard_map/ppermute | solution.py:389
  85.3 42.0 %collective-permute-start.10 = (bf16[4,32,5120]{2,1,0:T(8,128)(2,1)}, bf16[4,32,5120]{2,1,0:T(8,128)(2,1)S(1)}, u32[]{:S(2)}, u32[]{:S(2)}) collective-permute-start(bf16[4,32,5120]{2,1,0:T(8,128)(2,1)} %bitcast.10.refs_1_), channel_id=1, source_target_pairs={{0,4},{1,5},{2,6},{3,7},{4,0},{5,1},{6,2},{7,3},{8,12},{9,13},{10,... | collective-permute-start | bytes 3932168 | tf_op jit(solution)/shard_map/ppermute | solution.py:389
  127.3 33.2 %collective-permute-start.13 = (bf16[4,32,5120]{2,1,0:T(8,128)(2,1)}, bf16[4,32,5120]{2,1,0:T(8,128)(2,1)}, u32[]{:S(2)}, u32[]{:S(2)}) collective-permute-start(bf16[4,32,5120]{2,1,0:T(8,128)(2,1)} %bitcast.10.refs_1_), channel_id=1, source_target_pairs={{0,1},{1,0},{2,3},{3,2},{4,5},{5,4},{6,7},{7,6},{8,9},{9,8},{10,11... | collective-permute-start | bytes 3932168 | tf_op jit(solution)/shard_map/ppermute | solution.py:389
  130.1 25.0 %collective-permute-start.11 = (bf16[2,32,5120]{2,1,0:T(8,128)(2,1)}, bf16[2,32,5120]{2,1,0:T(8,128)(2,1)S(1)}, u32[]{:S(2)}, u32[]{:S(2)}) collective-permute-start(bf16[2,32,5120]{2,1,0:T(8,128)(2,1)} %part_of.6), channel_id=1, source_target_pairs={{0,2},{1,3},{2,0},{3,1},{4,6},{5,7},{6,4},{7,5},{8,10},{9,11},{10,... | collective-permute-start | bytes 1966088 | tf_op jit(solution)/shard_map/ppermute | solution.py:389
  133.7 21.6 %collective-permute-start.12 = (bf16[2,32,5120]{2,1,0:T(8,128)(2,1)}, bf16[2,32,5120]{2,1,0:T(8,128)(2,1)}, u32[]{:S(2)}, u32[]{:S(2)}) collective-permute-start(bf16[2,32,5120]{2,1,0:T(8,128)(2,1)} %part_of.7), channel_id=1, source_target_pairs={{0,4},{1,5},{2,6},{3,7},{4,0},{5,1},{6,2},{7,3},{8,12},{9,13},{10,... | collective-permute-start | bytes 1966088 | tf_op jit(solution)/shard_map/ppermute | solution.py:389
  135.0 25.6 %collective-permute-start.14 = (bf16[4,32,5120]{2,1,0:T(8,128)(2,1)S(1)}, bf16[4,32,5120]{2,1,0:T(8,128)(2,1)}, u32[]{:S(2)}, u32[]{:S(2)}) collective-permute-start(bf16[4,32,5120]{2,1,0:T(8,128)(2,1)S(1)} %collective-permute-done.9.refs_0_.refs_2_), channel_id=1, source_target_pairs={{0,1},{1,0},{2,3},{3,2},{4,5},{5,4},{6,7},{7,6},{8,9},{9,8},{10,11... | collective-permute-start | bytes 3932168 | tf_op jit(solution)/shard_map/ppermute | solution.py:389
  135.0 26.0 %collective-permute-start.15 = (bf16[4,32,5120]{2,1,0:T(8,128)(2,1)S(1)}, bf16[4,32,5120]{2,1,0:T(8,128)(2,1)}, u32[]{:S(2)}, u32[]{:S(2)}) collective-permute-start(bf16[4,32,5120]{2,1,0:T(8,128)(2,1)S(1)} %collective-permute-done.10.refs_0_.refs_3_), channel_id=1, source_target_pairs={{0,1},{1,0},{2,3},{3,2},{4,5},{5,4},{6,7},{7,6},{8,9},{9,8},{10,11... | collective-permute-start | bytes 3932168 | tf_op jit(solution)/shard_map/ppermute | solution.py:389
  160.5 56.7 %collective-permute-start.22 = (bf16[4,32,4096]{2,1,0:T(8,128)(2,1)S(1)}, bf16[4,32,4096]{2,1,0:T(8,128)(2,1)}, u32[]{:S(2)}, u32[]{:S(2)}) collective-permute-start(bf16[4,32,4096]{2,1,0:T(8,128)(2,1)S(1)} %copy-done.23), channel_id=1, source_target_pairs={{0,1},{1,0},{2,3},{3,2},{4,5},{5,4},{6,7},{7,6},{8,9},{9,8},{10,11... | collective-permute-start | bytes 3145736 | tf_op jit(solution)/shard_map/ppermute | solution.py:389
  160.6 56.8 %collective-permute-start.23 = (bf16[4,32,4096]{2,1,0:T(8,128)(2,1)}, bf16[4,32,4096]{2,1,0:T(8,128)(2,1)}, u32[]{:S(2)}, u32[]{:S(2)}) collective-permute-start(bf16[4,32,4096]{2,1,0:T(8,128)(2,1)} %collective-permute-done.18.refs_0_.refs_2_), channel_id=1, source_target_pairs={{0,1},{1,0},{2,3},{3,2},{4,5},{5,4},{6,7},{7,6},{8,9},{9,8},{10,11... | collective-permute-start | bytes 3145736 | tf_op jit(solution)/shard_map/ppermute | solution.py:389
  161.0 57.2 %collective-permute-start.24 = (bf16[4,32,4096]{2,1,0:T(8,128)(2,1)}, bf16[4,32,4096]{2,1,0:T(8,128)(2,1)}, u32[]{:S(2)}, u32[]{:S(2)}) collective-permute-start(bf16[4,32,4096]{2,1,0:T(8,128)(2,1)} %collective-permute-done.19.refs_0_.refs_3_), channel_id=1, source_target_pairs={{0,1},{1,0},{2,3},{3,2},{4,5},{5,4},{6,7},{7,6},{8,9},{9,8},{10,11... | collective-permute-start | bytes 3145736 | tf_op jit(solution)/shard_map/ppermute | solution.py:389
  187.4 28.8 %collective-permute-start.20 = (bf16[2,32,4096]{2,1,0:T(8,128)(2,1)S(1)}, bf16[2,32,4096]{2,1,0:T(8,128)(2,1)}, u32[]{:S(2)}, u32[]{:S(2)}) collective-permute-start(bf16[2,32,4096]{2,1,0:T(8,128)(2,1)S(1)} %part_of.8), channel_id=1, source_target_pairs={{0,2},{1,3},{2,0},{3,1},{4,6},{5,7},{6,4},{7,5},{8,10},{9,11},{10,... | collective-permute-start | bytes 1572872 | tf_op jit(solution)/shard_map/ppermute | solution.py:389
  191.1 25.2 %collective-permute-start.21 = (bf16[2,32,4096]{2,1,0:T(8,128)(2,1)S(1)}, bf16[2,32,4096]{2,1,0:T(8,128)(2,1)}, u32[]{:S(2)}, u32[]{:S(2)}) collective-permute-start(bf16[2,32,4096]{2,1,0:T(8,128)(2,1)S(1)} %part_of.9), channel_id=1, source_target_pairs={{0,4},{1,5},{2,6},{3,7},{4,0},{5,1},{6,2},{7,3},{8,12},{9,13},{10,... | collective-permute-start | bytes 1572872 | tf_op jit(solution)/shard_map/ppermute | solution.py:389
  217.2 39.5 %collective-permute-start.37 = (bf16[512,1024]{1,0:T(8,128)(2,1)}, bf16[512,1024]{1,0:T(8,128)(2,1)S(1)}, u32[]{:S(2)}, u32[]{:S(2)}) collective-permute-start(bf16[512,1024]{1,0:T(8,128)(2,1)} %get-tuple-element.90.refs_9_.refs_0_), channel_id=1, source_target_pairs={{0,1},{1,0},{2,3},{3,2},{4,5},{5,4},{6,7},{7,6},{8,9},{9,8},{10,11... | collective-permute-start | bytes 3145736 | tf_op jit(solution)/shard_map/ppermute | solution.py:389
  217.4 30.8 %collective-permute-start.27 = (bf16[4,32,4096]{2,1,0:T(8,128)(2,1)}, bf16[4,32,4096]{2,1,0:T(8,128)(2,1)S(1)}, u32[]{:S(2)}, u32[]{:S(2)}) collective-permute-start(bf16[4,32,4096]{2,1,0:T(8,128)(2,1)} %bitcast.150), channel_id=1, source_target_pairs={{0,2},{1,3},{2,0},{3,1},{4,6},{5,7},{6,4},{7,5},{8,10},{9,11},{10,... | collective-permute-start | bytes 3145736 | tf_op jit(solution)/shard_map/ppermute | solution.py:389
  218.2 28.2 %collective-permute-start.28 = (bf16[4,32,4096]{2,1,0:T(8,128)(2,1)}, bf16[4,32,4096]{2,1,0:T(8,128)(2,1)S(1)}, u32[]{:S(2)}, u32[]{:S(2)}) collective-permute-start(bf16[4,32,4096]{2,1,0:T(8,128)(2,1)} %bitcast.151), channel_id=1, source_target_pairs={{0,4},{1,5},{2,6},{3,7},{4,0},{5,1},{6,2},{7,3},{8,12},{9,13},{10,... | collective-permute-start | bytes 3145736 | tf_op jit(solution)/shard_map/ppermute | solution.py:389
  219.5 55.6 %collective-permute-start.31 = (bf16[4,32,4096]{2,1,0:T(8,128)(2,1)}, bf16[4,32,4096]{2,1,0:T(8,128)(2,1)S(1)}, u32[]{:S(2)}, u32[]{:S(2)}) collective-permute-start(bf16[4,32,4096]{2,1,0:T(8,128)(2,1)} %bitcast.152), channel_id=1, source_target_pairs={{0,1},{1,0},{2,3},{3,2},{4,5},{5,4},{6,7},{7,6},{8,9},{9,8},{10,11... | collective-permute-start | bytes 3145736 | tf_op jit(solution)/shard_map/ppermute | solution.py:389
  243.7 18.9 %collective-permute-start.36 = (bf16[512,2048]{1,0:T(8,128)(2,1)S(1)}, bf16[512,2048]{1,0:T(8,128)(2,1)S(1)}, u32[]{:S(2)}, u32[]{:S(2)}) collective-permute-start(bf16[512,2048]{1,0:T(8,128)(2,1)S(1)} %constant_dynamic-slice_fusion), channel_id=1, source_target_pairs={{0,1},{1,0},{2,3},{3,2},{4,5},{5,4},{6,7},{7,6},{8,9},{9,8},{10,11... | collective-permute-start | bytes 6291464 | tf_op jit(solution)/shard_map/ppermute | solution.py:389
  246.6 14.4 %collective-permute-start.29 = (bf16[2,32,4096]{2,1,0:T(8,128)(2,1)S(1)}, bf16[2,32,4096]{2,1,0:T(8,128)(2,1)S(1)}, u32[]{:S(2)}, u32[]{:S(2)}) collective-permute-start(bf16[2,32,4096]{2,1,0:T(8,128)(2,1)S(1)} %part_of.10), channel_id=1, source_target_pairs={{0,2},{1,3},{2,0},{3,1},{4,6},{5,7},{6,4},{7,5},{8,10},{9,11},{10,... | collective-permute-start | bytes 1572872 | tf_op jit(solution)/shard_map/ppermute | solution.py:389
  248.5 14.1 %collective-permute-start.30 = (bf16[2,32,4096]{2,1,0:T(8,128)(2,1)S(1)}, bf16[2,32,4096]{2,1,0:T(8,128)(2,1)S(1)}, u32[]{:S(2)}, u32[]{:S(2)}) collective-permute-start(bf16[2,32,4096]{2,1,0:T(8,128)(2,1)S(1)} %part_of.11), channel_id=1, source_target_pairs={{0,4},{1,5},{2,6},{3,7},{4,0},{5,1},{6,2},{7,3},{8,12},{9,13},{10,... | collective-permute-start | bytes 1572872 | tf_op jit(solution)/shard_map/ppermute | solution.py:389
  256.8 18.4 %collective-permute-start.32 = (bf16[4,32,4096]{2,1,0:T(8,128)(2,1)S(1)}, bf16[4,32,4096]{2,1,0:T(8,128)(2,1)S(1)}, u32[]{:S(2)}, u32[]{:S(2)}) collective-permute-start(bf16[4,32,4096]{2,1,0:T(8,128)(2,1)S(1)} %collective-permute-done.27.refs_0_.refs_2_), channel_id=1, source_target_pairs={{0,1},{1,0},{2,3},{3,2},{4,5},{5,4},{6,7},{7,6},{8,9},{9,8},{10,11... | collective-permute-start | bytes 3145736 | tf_op jit(solution)/shard_map/ppermute | solution.py:389
  261.1 14.6 %collective-permute-start.33 = (bf16[4,32,4096]{2,1,0:T(8,128)(2,1)S(1)}, bf16[4,32,4096]{2,1,0:T(8,128)(2,1)}, u32[]{:S(2)}, u32[]{:S(2)}) collective-permute-start(bf16[4,32,4096]{2,1,0:T(8,128)(2,1)S(1)} %collective-permute-done.28.refs_0_.refs_3_), channel_id=1, source_target_pairs={{0,1},{1,0},{2,3},{3,2},{4,5},{5,4},{6,7},{7,6},{8,9},{9,8},{10,11... | collective-permute-start | bytes 3145736 | tf_op jit(solution)/shard_map/ppermute | solution.py:389
  262.6 13.5 %collective-permute-start.34 = (bf16[2,32,4096]{2,1,0:T(8,128)(2,1)S(1)}, bf16[2,32,4096]{2,1,0:T(8,128)(2,1)S(1)}, u32[]{:S(2)}, u32[]{:S(2)}) collective-permute-start(bf16[2,32,4096]{2,1,0:T(8,128)(2,1)S(1)} %collective-permute-done.29.refs_4_), channel_id=1, source_target_pairs={{0,1},{1,0},{2,3},{3,2},{4,5},{5,4},{6,7},{7,6},{8,9},{9,8},{10,11... | collective-permute-start | bytes 1572872 | tf_op jit(solution)/shard_map/ppermute | solution.py:389
  262.6 14.3 %collective-permute-start.35 = (bf16[2,32,4096]{2,1,0:T(8,128)(2,1)S(1)}, bf16[2,32,4096]{2,1,0:T(8,128)(2,1)S(1)}, u32[]{:S(2)}, u32[]{:S(2)}) collective-permute-start(bf16[2,32,4096]{2,1,0:T(8,128)(2,1)S(1)} %collective-permute-done.30.refs_5_), channel_id=1, source_target_pairs={{0,1},{1,0},{2,3},{3,2},{4,5},{5,4},{6,7},{7,6},{8,9},{9,8},{10,11... | collective-permute-start | bytes 1572872 | tf_op jit(solution)/shard_map/ppermute | solution.py:389
  275.1 62.7 %collective-permute-start.41 = (bf16[512,512]{1,0:T(8,128)(2,1)}, bf16[512,512]{1,0:T(8,128)(2,1)}, u32[]{:S(2)}, u32[]{:S(2)}) collective-permute-start(bf16[512,512]{1,0:T(8,128)(2,1)} %get-tuple-element.126), channel_id=1, source_target_pairs={{0,1},{1,0},{2,3},{3,2},{4,5},{5,4},{6,7},{7,6},{8,9},{9,8},{10,11... | collective-permute-start | bytes 1572872 | tf_op jit(solution)/shard_map/ppermute | solution.py:389
  275.2 84.6 %collective-permute-start.47 = (bf16[512,512]{1,0:T(8,128)(2,1)}, bf16[512,512]{1,0:T(8,128)(2,1)}, u32[]{:S(2)}, u32[]{:S(2)}) collective-permute-start(bf16[512,512]{1,0:T(8,128)(2,1)} %get-tuple-element.124), channel_id=1, source_target_pairs={{0,1},{1,0},{2,3},{3,2},{4,5},{5,4},{6,7},{7,6},{8,9},{9,8},{10,11... | collective-permute-start | bytes 1572872 | tf_op jit(solution)/shard_map/ppermute | solution.py:389
  275.6 32.6 %collective-permute-start.40 = (bf16[2,32,4096]{2,1,0:T(8,128)(2,1)}, bf16[2,32,4096]{2,1,0:T(8,128)(2,1)S(1)}, u32[]{:S(2)}, u32[]{:S(2)}) collective-permute-start(bf16[2,32,4096]{2,1,0:T(8,128)(2,1)} %get-tuple-element.112), channel_id=1, source_target_pairs={{0,2},{1,3},{2,0},{3,1},{4,6},{5,7},{6,4},{7,5},{8,10},{9,11},{10,... | collective-permute-start | bytes 1572872 | tf_op jit(solution)/shard_map/ppermute | solution.py:389
  276.1 32.9 %collective-permute-start.39 = (bf16[2,32,4096]{2,1,0:T(8,128)(2,1)}, bf16[2,32,4096]{2,1,0:T(8,128)(2,1)}, u32[]{:S(2)}, u32[]{:S(2)}) collective-permute-start(bf16[2,32,4096]{2,1,0:T(8,128)(2,1)} %get-tuple-element.114), channel_id=1, source_target_pairs={{0,4},{1,5},{2,6},{3,7},{4,0},{5,1},{6,2},{7,3},{8,12},{9,13},{10,... | collective-permute-start | bytes 1572872 | tf_op jit(solution)/shard_map/ppermute | solution.py:389
  304.7 33.6 %collective-permute-start.42 = (bf16[512,4096]{1,0:T(8,128)(2,1)}, bf16[512,4096]{1,0:T(8,128)(2,1)}, u32[]{:S(2)}, u32[]{:S(2)}) collective-permute-start(bf16[512,4096]{1,0:T(8,128)(2,1)} %get-tuple-element.41), channel_id=1, source_target_pairs={{0,1},{1,0},{2,3},{3,2},{4,5},{5,4},{6,7},{7,6},{8,9},{9,8},{10,11... | collective-permute-start | bytes 12582920 | tf_op jit(solution)/shard_map/ppermute | solution.py:389
  310.5 25.0 %collective-permute-start.54 = (bf16[4,32,4096]{2,1,0:T(8,128)(2,1)S(1)}, bf16[4,32,4096]{2,1,0:T(8,128)(2,1)S(1)}, u32[]{:S(2)}, u32[]{:S(2)}) collective-permute-start(bf16[4,32,4096]{2,1,0:T(8,128)(2,1)S(1)} %pad_maximum_fusion.6.refs_8_), channel_id=1, source_target_pairs={{0,4},{1,5},{2,6},{3,7},{4,0},{5,1},{6,2},{7,3},{8,12},{9,13},{10,... | collective-permute-start | bytes 3145736 | tf_op jit(solution)/shard_map/ppermute | solution.py:389
  311.9 24.4 %collective-permute-start.53 = (bf16[4,32,4096]{2,1,0:T(8,128)(2,1)S(1)}, bf16[4,32,4096]{2,1,0:T(8,128)(2,1)S(1)}, u32[]{:S(2)}, u32[]{:S(2)}) collective-permute-start(bf16[4,32,4096]{2,1,0:T(8,128)(2,1)S(1)} %pad_maximum_fusion.5.refs_7_), channel_id=1, source_target_pairs={{0,2},{1,3},{2,0},{3,1},{4,6},{5,7},{6,4},{7,5},{8,10},{9,11},{10,... | collective-permute-start | bytes 3145736 | tf_op jit(solution)/shard_map/ppermute | solution.py:389
  335.5 24.7 %collective-permute-start.49 = (bf16[512,512]{1,0:T(8,128)(2,1)}, bf16[512,512]{1,0:T(8,128)(2,1)}, u32[]{:S(2)}, u32[]{:S(2)}) collective-permute-start(bf16[512,512]{1,0:T(8,128)(2,1)} %get-tuple-element.122), channel_id=1, source_target_pairs={{0,1},{1,0},{2,3},{3,2},{4,5},{5,4},{6,7},{7,6},{8,9},{9,8},{10,11... | collective-permute-start | bytes 1572872 | tf_op jit(solution)/shard_map/ppermute | solution.py:389
  336.2 25.9 %collective-permute-start.52 = (bf16[2,592,1024]{2,1,0:T(8,128)(2,1)}, bf16[2,592,1024]{2,1,0:T(8,128)(2,1)}, u32[]{:S(2)}, u32[]{:S(2)}) collective-permute-start(bf16[2,592,1024]{2,1,0:T(8,128)(2,1)} %pad_maximum_fusion.2.refs_10_), channel_id=1, source_target_pairs={{0,1},{1,0},{2,3},{3,2},{4,5},{5,4},{6,7},{7,6},{8,9},{9,8},{10,11... | collective-permute-start | bytes 7274504 | tf_op jit(solution)/shard_map/ppermute | solution.py:389
  337.7 194.1 %reduce-scatter.9.cloned.1.call-start = ((), (), s32[]{:S(2)}) async-start(), calls=%async_computation.7 | async-start | bytes 1310720 | tf_op jit(solution)/shard_map/reduce_scatter | solution.py:711
  337.8 23.9 %collective-permute-start.48 = (bf16[512,1024]{1,0:T(8,128)(2,1)S(1)}, bf16[512,1024]{1,0:T(8,128)(2,1)S(1)}, u32[]{:S(2)}, u32[]{:S(2)}) collective-permute-start(bf16[512,1024]{1,0:T(8,128)(2,1)S(1)} %get-tuple-element.37), channel_id=1, source_target_pairs={{0,1},{1,0},{2,3},{3,2},{4,5},{5,4},{6,7},{7,6},{8,9},{9,8},{10,11... | collective-permute-start | bytes 3145736 | tf_op jit(solution)/shard_map/ppermute | solution.py:389
  338.4 23.8 %collective-permute-start.50 = (bf16[512,1024]{1,0:T(8,128)(2,1)S(1)}, bf16[512,1024]{1,0:T(8,128)(2,1)S(1)}, u32[]{:S(2)}, u32[]{:S(2)}) collective-permute-start(bf16[512,1024]{1,0:T(8,128)(2,1)S(1)} %get-tuple-element.39.refs_4_), channel_id=1, source_target_pairs={{0,1},{1,0},{2,3},{3,2},{4,5},{5,4},{6,7},{7,6},{8,9},{9,8},{10,11... | collective-permute-start | bytes 3145736 | tf_op jit(solution)/shard_map/ppermute | solution.py:389
  359.7 81.4 %collective-permute-start.38 = (bf16[512,512]{1,0:T(8,128)(2,1)}, bf16[512,512]{1,0:T(8,128)(2,1)S(1)}, u32[]{:S(2)}, u32[]{:S(2)}) collective-permute-start(bf16[512,512]{1,0:T(8,128)(2,1)} %get-tuple-element.120), channel_id=1, source_target_pairs={{0,1},{1,0},{2,3},{3,2},{4,5},{5,4},{6,7},{7,6},{8,9},{9,8},{10,11... | collective-permute-start | bytes 1572872 | tf_op jit(solution)/shard_map/ppermute | solution.py:389
  360.1 21.0 %collective-permute-start.46 = (bf16[2,32,4096]{2,1,0:T(8,128)(2,1)}, bf16[2,32,4096]{2,1,0:T(8,128)(2,1)S(1)}, u32[]{:S(2)}, u32[]{:S(2)}) collective-permute-start(bf16[2,32,4096]{2,1,0:T(8,128)(2,1)} %get-tuple-element.106), channel_id=1, source_target_pairs={{0,2},{1,3},{2,0},{3,1},{4,6},{5,7},{6,4},{7,5},{8,10},{9,11},{10,... | collective-permute-start | bytes 1572872 | tf_op jit(solution)/shard_map/ppermute | solution.py:389
  361.7 19.5 %collective-permute-start.45 = (bf16[2,32,4096]{2,1,0:T(8,128)(2,1)}, bf16[2,32,4096]{2,1,0:T(8,128)(2,1)S(1)}, u32[]{:S(2)}, u32[]{:S(2)}) collective-permute-start(bf16[2,32,4096]{2,1,0:T(8,128)(2,1)} %get-tuple-element.108), channel_id=1, source_target_pairs={{0,4},{1,5},{2,6},{3,7},{4,0},{5,1},{6,2},{7,3},{8,12},{9,13},{10,... | collective-permute-start | bytes 1572872 | tf_op jit(solution)/shard_map/ppermute | solution.py:389
  377.8 34.8 %collective-permute-start.57 = (bf16[2,32,4096]{2,1,0:T(8,128)(2,1)}, bf16[2,32,4096]{2,1,0:T(8,128)(2,1)S(1)}, u32[]{:S(2)}, u32[]{:S(2)}) collective-permute-start(bf16[2,32,4096]{2,1,0:T(8,128)(2,1)} %get-tuple-element.100), channel_id=1, source_target_pairs={{0,2},{1,3},{2,0},{3,1},{4,6},{5,7},{6,4},{7,5},{8,10},{9,11},{10,... | collective-permute-start | bytes 1572872 | tf_op jit(solution)/shard_map/ppermute | solution.py:389
  378.8 35.1 %collective-permute-start.56 = (bf16[2,32,4096]{2,1,0:T(8,128)(2,1)}, bf16[2,32,4096]{2,1,0:T(8,128)(2,1)S(1)}, u32[]{:S(2)}, u32[]{:S(2)}) collective-permute-start(bf16[2,32,4096]{2,1,0:T(8,128)(2,1)} %get-tuple-element.102), channel_id=1, source_target_pairs={{0,4},{1,5},{2,6},{3,7},{4,0},{5,1},{6,2},{7,3},{8,12},{9,13},{10,... | collective-permute-start | bytes 1572872 | tf_op jit(solution)/shard_map/ppermute | solution.py:389
  382.4 35.8 %collective-permute-start.59 = (bf16[4,32,4096]{2,1,0:T(8,128)(2,1)}, bf16[4,32,4096]{2,1,0:T(8,128)(2,1)}, u32[]{:S(2)}, u32[]{:S(2)}) collective-permute-start(bf16[4,32,4096]{2,1,0:T(8,128)(2,1)} %pad_maximum_fusion.8.refs_8_), channel_id=1, source_target_pairs={{0,4},{1,5},{2,6},{3,7},{4,0},{5,1},{6,2},{7,3},{8,12},{9,13},{10,... | collective-permute-start | bytes 3145736 | tf_op jit(solution)/shard_map/ppermute | solution.py:389
  400.5 43.2 %collective-permute-start.55 = (bf16[3,512,1024]{2,1,0:T(8,128)(2,1)}, bf16[3,512,1024]{2,1,0:T(8,128)(2,1)}, u32[]{:S(2)}, u32[]{:S(2)}) collective-permute-start(bf16[3,512,1024]{2,1,0:T(8,128)(2,1)} %pad_maximum_fusion.1.refs_6_.refs_0_), channel_id=1, source_target_pairs={{0,1},{1,0},{2,3},{3,2},{4,5},{5,4},{6,7},{7,6},{8,9},{9,8},{10,11... | collective-permute-start | bytes 9437192 | tf_op jit(solution)/shard_map/ppermute | solution.py:389
  412.9 25.4 %collective-permute-start.58 = (bf16[4,32,4096]{2,1,0:T(8,128)(2,1)S(1)}, bf16[4,32,4096]{2,1,0:T(8,128)(2,1)S(1)}, u32[]{:S(2)}, u32[]{:S(2)}) collective-permute-start(bf16[4,32,4096]{2,1,0:T(8,128)(2,1)S(1)} %copy-done.53), channel_id=1, source_target_pairs={{0,2},{1,3},{2,0},{3,1},{4,6},{5,7},{6,4},{7,5},{8,10},{9,11},{10,... | collective-permute-start | bytes 3145736 | tf_op jit(solution)/shard_map/ppermute | solution.py:389
  417.8 24.9 %collective-permute-start.43 = (bf16[512,1024]{1,0:T(8,128)(2,1)S(1)}, bf16[512,1024]{1,0:T(8,128)(2,1)S(1)}, u32[]{:S(2)}, u32[]{:S(2)}) collective-permute-start(bf16[512,1024]{1,0:T(8,128)(2,1)S(1)} %copy-done.13), channel_id=1, source_target_pairs={{0,1},{1,0},{2,3},{3,2},{4,5},{5,4},{6,7},{7,6},{8,9},{9,8},{10,11... | collective-permute-start | bytes 3145736 | tf_op jit(solution)/shard_map/ppermute | solution.py:389
  418.2 23.7 %collective-permute-start.44 = (bf16[512,512]{1,0:T(8,128)(2,1)S(1)}, bf16[512,512]{1,0:T(8,128)(2,1)S(1)}, u32[]{:S(2)}, u32[]{:S(2)}) collective-permute-start(bf16[512,512]{1,0:T(8,128)(2,1)S(1)} %copy-done.55), channel_id=1, source_target_pairs={{0,1},{1,0},{2,3},{3,2},{4,5},{5,4},{6,7},{7,6},{8,9},{9,8},{10,11... | collective-permute-start | bytes 1572872 | tf_op jit(solution)/shard_map/ppermute | solution.py:389
  461.1 15.5 %collective-permute-start.61 = (bf16[2,32,4224]{2,1,0:T(8,128)(2,1)}, bf16[2,32,4224]{2,1,0:T(8,128)(2,1)}, u32[]{:S(2)}, u32[]{:S(2)}) collective-permute-start(bf16[2,32,4224]{2,1,0:T(8,128)(2,1)} %get-tuple-element.95), channel_id=1, source_target_pairs={{0,4},{1,5},{2,6},{3,7},{4,0},{5,1},{6,2},{7,3},{8,12},{9,13},{10,... | collective-permute-start | bytes 1622024 | tf_op jit(solution)/shard_map/ppermute | solution.py:389
  462.2 15.5 %collective-permute-start.63 = (bf16[2,32,4224]{2,1,0:T(8,128)(2,1)}, bf16[2,32,4224]{2,1,0:T(8,128)(2,1)}, u32[]{:S(2)}, u32[]{:S(2)}) collective-permute-start(bf16[2,32,4224]{2,1,0:T(8,128)(2,1)} %get-tuple-element.94), channel_id=1, source_target_pairs={{0,2},{1,3},{2,0},{3,1},{4,6},{5,7},{6,4},{7,5},{8,10},{9,11},{10,... | collective-permute-start | bytes 1622024 | tf_op jit(solution)/shard_map/ppermute | solution.py:389
  465.0 34.1 %collective-permute-start.66 = (bf16[4,32,4096]{2,1,0:T(8,128)(2,1)S(1)}, bf16[4,32,4096]{2,1,0:T(8,128)(2,1)}, u32[]{:S(2)}, u32[]{:S(2)}) collective-permute-start(bf16[4,32,4096]{2,1,0:T(8,128)(2,1)S(1)} %copy-done.42), channel_id=1, source_target_pairs={{0,4},{1,5},{2,6},{3,7},{4,0},{5,1},{6,2},{7,3},{8,12},{9,13},{10,... | collective-permute-start | bytes 3145736 | tf_op jit(solution)/shard_map/ppermute | solution.py:389
  465.5 34.6 %collective-permute-start.65 = (bf16[4,32,4096]{2,1,0:T(8,128)(2,1)S(1)}, bf16[4,32,4096]{2,1,0:T(8,128)(2,1)}, u32[]{:S(2)}, u32[]{:S(2)}) collective-permute-start(bf16[4,32,4096]{2,1,0:T(8,128)(2,1)S(1)} %pad_maximum_fusion.9.refs_8_), channel_id=1, source_target_pairs={{0,2},{1,3},{2,0},{3,1},{4,6},{5,7},{6,4},{7,5},{8,10},{9,11},{10,... | collective-permute-start | bytes 3145736 | tf_op jit(solution)/shard_map/ppermute | solution.py:389
  466.6 74.0 %reduce-scatter.7.cloned.1.call-start = ((), (), s32[]{:S(2)}) async-start(), calls=%async_computation.6 | async-start | bytes 1310720 | tf_op jit(solution)/shard_map/reduce_scatter | solution.py:711
  480.5 40.4 %collective-permute-start.64 = (bf16[4,32,4224]{2,1,0:T(8,128)(2,1)}, bf16[4,32,4224]{2,1,0:T(8,128)(2,1)}, u32[]{:S(2)}, u32[]{:S(2)}) collective-permute-start(bf16[4,32,4224]{2,1,0:T(8,128)(2,1)} %pad_maximum_fusion.4), channel_id=1, source_target_pairs={{0,4},{1,5},{2,6},{3,7},{4,0},{5,1},{6,2},{7,3},{8,12},{9,13},{10,... | collective-permute-start | bytes 3244040 | tf_op jit(solution)/shard_map/ppermute | solution.py:389
  482.5 39.1 %collective-permute-start.62 = (bf16[4,32,4224]{2,1,0:T(8,128)(2,1)}, bf16[4,32,4224]{2,1,0:T(8,128)(2,1)}, u32[]{:S(2)}, u32[]{:S(2)}) collective-permute-start(bf16[4,32,4224]{2,1,0:T(8,128)(2,1)} %pad_maximum_fusion.3), channel_id=1, source_target_pairs={{0,2},{1,3},{2,0},{3,1},{4,6},{5,7},{6,4},{7,5},{8,10},{9,11},{10,... | collective-permute-start | bytes 3244040 | tf_op jit(solution)/shard_map/ppermute | solution.py:389
  503.2 57.0 %reduce-scatter.5.cloned.1.call-start = ((), (), s32[]{:S(2)}) async-start(), calls=%async_computation.5 | async-start | bytes 1351680 | tf_op jit(solution)/shard_map/reduce_scatter | solution.py:711
  (79 other events, 497.9 us)
Sparse Core Ops, SparseCore 0:
  11.6 37.4 all-gather.6
  51.2 32.5 all-gather.8
  85.4 26.9 all-gather.10
  337.8 28.2 reduce-scatter.10
  466.7 28.5 reduce-scatter.8
  503.3 28.0 reduce-scatter.6
  533.9 26.2 reduce-scatter.4
